TPU v7x, 32 devices: a whole 2x2x4 slice. The times are simulated.
32 devices in a mesh: dp: 8 (over y, x, core), mp: 4 (over z).
Axes of the slice: x: 2, y: 2, z: 4, core: 2. Of those that a mesh axis runs over, the one named last changes fastest.
Arguments:
- tokens: bfloat16 [16384, 768], P('dp'), may hold values from -6 to 6
- lengths: int32 [8, 16], P('dp'), may hold values from 1 to 1024, 2048 in all within a row
- first_gain: bfloat16 [768], P('dp'), may hold values from 0.5 to 1.5
- first_shift: bfloat16 [768], P('dp'), may hold values from -1.25 to 1.25
- qkv_weight: bfloat16 [3, 768, 768], P(None, 'dp', 'mp'), may hold values from -0.21875 to 0.21875
- qv_bias: bfloat16 [2, 4, 192], P(None, 'mp', 'dp'), may hold values from -1.25 to 1.25
- proj_weight: bfloat16 [768, 768], P('mp', 'dp'), may hold values from -0.875 to 0.875
- proj_bias: bfloat16 [768], P('dp'), may hold values from -1.25 to 1.25
- second_gain: bfloat16 [768], P('dp'), may hold values from 0.5 to 1.5
- second_shift: bfloat16 [768], P('dp'), may hold values from -1.25 to 1.25
- fc_weight: bfloat16 [768, 3072], P('dp', 'mp'), may hold values from -0.21875 to 0.21875
- fc_bias: bfloat16 [4, 768], P('mp', 'dp'), may hold values from -1.25 to 1.25
- out_weight: bfloat16 [3072, 768], P('mp', 'dp'), may hold values from -0.15625 to 0.15625
- out_bias: bfloat16 [768], P('dp'), may hold values from -1.25 to 1.25
- out_grad: bfloat16 [16384, 768], P('dp'), may hold values from -6 to 6
Outputs:
- output: bfloat16 [16384, 768], P('dp')
- grad_tokens: bfloat16 [16384, 768], P('dp')
- grad_first_gain: float32 [768], P('dp')
- grad_first_shift: float32 [768], P('dp')
- grad_qkv_weight: float32 [3, 768, 768], P(None, 'dp', 'mp')
- grad_qv_bias: float32 [2, 4, 192], P(None, 'mp', 'dp')
- grad_proj_weight: float32 [768, 768], P('mp', 'dp')
- grad_proj_bias: float32 [768], P('dp')
- grad_second_gain: float32 [768], P('dp')
- grad_second_shift: float32 [768], P('dp')
- grad_fc_weight: float32 [768, 3072], P('dp', 'mp')
- grad_fc_bias: float32 [4, 768], P('mp', 'dp')
- grad_out_weight: float32 [3072, 768], P('mp', 'dp')
- grad_out_bias: float32 [768], P('dp')
Inputs may be any that keep to these rules, and one draw needn't show every extreme that they name: `lengths`: each row sums to 2048 and its largest entry is 1024.
All inputs are finite; a program needn't handle non-finite values.
Results may differ from a plain program's by a relative error of at most 0.018.
Values may be sent and summed in bfloat16 or wider, within the bound.
A program may use at most 128 MiB of HBM per device.

v0:
```python
import jax
import jax.numpy as jnp
from jax import lax
from jax.sharding import PartitionSpec as P

HD = 64
MAXLEN = 1024
QBLOCK = 512


EPS = 1e-05
SCALE = 0.125
NEG = -1e30
GELU_C = 0.7978845608028654


def split_up(shard, dim, size):
    before, after = (shard.shape[:dim], shard.shape[dim + 1 :])
    return jnp.moveaxis(shard.reshape(*before, size, -1, *after), dim, 0)


def summed_on_arrival(shard, axis, dim):
    size = lax.axis_size(axis)
    pieces = lax.all_to_all(split_up(shard, dim, size), axis, 0, 0, tiled=True)
    return jnp.sum(pieces.astype(jnp.float32), axis=0)


def norm_parts(values):
    mean = jnp.mean(values, axis=-1, keepdims=True)
    centred = values - mean
    inverse = lax.rsqrt(jnp.mean(centred * centred, axis=-1, keepdims=True) + EPS)
    return (centred * inverse, inverse)


def norm_back(grad, gain, normed, inverse):
    scaled = grad * gain
    return inverse * (
        scaled
        - jnp.mean(scaled, axis=-1, keepdims=True)
        - normed * jnp.mean(scaled * normed, axis=-1, keepdims=True)
    )


def gelu_tanh(values):
    return 0.5 * values * (1.0 + jnp.tanh(GELU_C * (values + 0.044715 * values * values * values)))


def gelu_slope(values):
    inner = GELU_C * (values + 0.044715 * values * values * values)
    tangent = jnp.tanh(inner)
    return 0.5 * (1.0 + tangent) + 0.5 * values * (1.0 - tangent * tangent) * GELU_C * (
        1.0 + 3.0 * 0.044715 * values * values
    )


def segment_ids(lengths_row, count):
    ends = jnp.cumsum(lengths_row)
    places = jnp.arange(count, dtype=jnp.int32)
    return jnp.sum((places[:, None] >= ends[None, :]).astype(jnp.int32), axis=1)


def padded(array, span, fill):
    front = jnp.full((span,) + array.shape[1:], fill, array.dtype)
    return jnp.concatenate([front, array], axis=0)


def block_scores(query, keys_pad, seg, seg_pad, index):
    start = index * QBLOCK
    q_rows = lax.dynamic_slice_in_dim(query, start, QBLOCK, 0)
    k_rows = lax.dynamic_slice_in_dim(keys_pad, start, QBLOCK + MAXLEN, 0)
    q_seg = lax.dynamic_slice_in_dim(seg, start, QBLOCK, 0)
    k_seg = lax.dynamic_slice_in_dim(seg_pad, start, QBLOCK + MAXLEN, 0)
    q_place = start + jnp.arange(QBLOCK, dtype=jnp.int32)
    k_place = start - MAXLEN + jnp.arange(QBLOCK + MAXLEN, dtype=jnp.int32)
    allowed = (q_seg[:, None] == k_seg[None, :]) & (k_place[None, :] <= q_place[:, None])
    scores = jnp.einsum("qhd,khd->hqk", q_rows, k_rows, preferred_element_type=jnp.float32) * SCALE
    return (jnp.where(allowed[None], scores, NEG), q_rows, k_rows)


def attend_forward(query, keys, values, seg):
    count, heads, size = query.shape
    keys_pad = padded(keys, MAXLEN, 0)
    values_pad = padded(values, MAXLEN, 0)
    seg_pad = padded(seg, MAXLEN, -1)

    def one_block(index):
        masked, q_rows, k_rows = block_scores(query, keys_pad, seg, seg_pad, index)
        v_rows = lax.dynamic_slice_in_dim(values_pad, index * QBLOCK, QBLOCK + MAXLEN, 0)
        biggest = jnp.max(masked, axis=-1, keepdims=True)
        expo = jnp.exp(masked - biggest)
        total = jnp.sum(expo, axis=-1, keepdims=True)
        probs = (expo / total).astype(jnp.bfloat16)
        block_out = jnp.einsum("hqk,khd->qhd", probs, v_rows, preferred_element_type=jnp.float32)
        return (block_out.astype(jnp.bfloat16), (biggest + jnp.log(total))[..., 0])

    outs, log_sums = lax.map(one_block, jnp.arange(count // QBLOCK, dtype=jnp.int32))
    return (outs.reshape(count, heads, size), log_sums)


def attend_backward(query, keys, values, seg, log_sums, rows_grad):
    count, heads, size = query.shape
    keys_pad = padded(keys, MAXLEN, 0)
    values_pad = padded(values, MAXLEN, 0)
    seg_pad = padded(seg, MAXLEN, -1)
    zeros = jnp.zeros((count + MAXLEN, heads, size), jnp.float32)

    def one_block(carry, index):
        key_acc, value_acc = carry
        start = index * QBLOCK
        masked, q_rows, k_rows = block_scores(query, keys_pad, seg, seg_pad, index)
        v_rows = lax.dynamic_slice_in_dim(values_pad, start, QBLOCK + MAXLEN, 0)
        g_rows = lax.dynamic_slice_in_dim(rows_grad, start, QBLOCK, 0)
        probs = jnp.exp(masked - log_sums[index][:, :, None])
        prob_grad = jnp.einsum("qhd,khd->hqk", g_rows, v_rows, preferred_element_type=jnp.float32)
        score_grad = (
            probs * (prob_grad - jnp.sum(probs * prob_grad, axis=-1, keepdims=True))
        ).astype(jnp.bfloat16)
        q_grad = (
            jnp.einsum("hqk,khd->qhd", score_grad, k_rows, preferred_element_type=jnp.float32)
            * SCALE
        )
        k_part = (
            jnp.einsum("hqk,qhd->khd", score_grad, q_rows, preferred_element_type=jnp.float32)
            * SCALE
        )
        v_part = jnp.einsum(
            "hqk,qhd->khd", probs.astype(jnp.bfloat16), g_rows, preferred_element_type=jnp.float32
        )
        key_acc = lax.dynamic_update_slice_in_dim(
            key_acc, lax.dynamic_slice_in_dim(key_acc, start, QBLOCK + MAXLEN, 0) + k_part, start, 0
        )
        value_acc = lax.dynamic_update_slice_in_dim(
            value_acc,
            lax.dynamic_slice_in_dim(value_acc, start, QBLOCK + MAXLEN, 0) + v_part,
            start,
            0,
        )
        return ((key_acc, value_acc), q_grad)

    (key_acc, value_acc), q_blocks = lax.scan(
        one_block, (zeros, zeros), jnp.arange(count // QBLOCK, dtype=jnp.int32)
    )
    query_grad = q_blocks.reshape(count, heads, size).astype(jnp.bfloat16)
    return (
        query_grad,
        key_acc[MAXLEN:].astype(jnp.bfloat16),
        value_acc[MAXLEN:].astype(jnp.bfloat16),
    )


def per_device(
    tokens,
    lengths,
    first_gain,
    first_shift,
    qkv_weight,
    qv_bias,
    proj_weight,
    proj_bias,
    second_gain,
    second_shift,
    fc_weight,
    fc_bias,
    out_weight,
    out_bias,
    out_grad,
):
    count = tokens.shape[0]
    seg = segment_ids(lengths[0], count)
    gain_one, shift_one, qkv_all, qv_all, proj_all, proj_bias_all = (
        lax.all_gather(first_gain, "dp", axis=0, tiled=True),
        lax.all_gather(first_shift, "dp", axis=0, tiled=True),
        lax.all_gather(qkv_weight, "dp", axis=1, tiled=True),
        lax.all_gather(qv_bias, "dp", axis=2, tiled=True),
        lax.all_gather(proj_weight, "dp", axis=1, tiled=True),
        lax.all_gather(proj_bias, "dp", axis=0, tiled=True),
    )
    gain_one_f = gain_one.astype(jnp.float32)
    xin = tokens.astype(jnp.float32)
    normed_one, inverse_one = norm_parts(xin)
    act_one = (normed_one * gain_one_f + shift_one.astype(jnp.float32)).astype(jnp.bfloat16)
    projected = jnp.einsum("td,cde->cte", act_one, qkv_all, preferred_element_type=jnp.float32)
    width = qkv_all.shape[2]
    heads = width // HD
    query = (
        (projected[0] + qv_all[0, 0].astype(jnp.float32))
        .astype(jnp.bfloat16)
        .reshape(count, heads, HD)
    )
    keys = projected[1].astype(jnp.bfloat16).reshape(count, heads, HD)
    values = (
        (projected[2] + qv_all[1, 0].astype(jnp.float32))
        .astype(jnp.bfloat16)
        .reshape(count, heads, HD)
    )
    attn_rows, log_sums = attend_forward(query, keys, values, seg)
    flat_rows = attn_rows.reshape(count, width)
    gain_two, shift_two, fc_all, fc_bias_all, out_all, out_bias_all = (
        lax.all_gather(second_gain, "dp", axis=0, tiled=True),
        lax.all_gather(second_shift, "dp", axis=0, tiled=True),
        lax.all_gather(fc_weight, "dp", axis=0, tiled=True),
        lax.all_gather(fc_bias, "dp", axis=1, tiled=True),
        lax.all_gather(out_weight, "dp", axis=1, tiled=True),
        lax.all_gather(out_bias, "dp", axis=0, tiled=True),
    )
    gain_two_f = gain_two.astype(jnp.float32)
    shift_two_f = shift_two.astype(jnp.float32)
    branch_one = lax.psum(
        jnp.dot(flat_rows, proj_all, preferred_element_type=jnp.float32).astype(jnp.bfloat16), "mp"
    ).astype(jnp.float32)
    hidden_one = xin + branch_one + proj_bias_all.astype(jnp.float32)
    normed_two, inverse_two = norm_parts(hidden_one)
    act_two = (normed_two * gain_two_f + shift_two_f).astype(jnp.bfloat16)
    pre = jnp.dot(act_two, fc_all, preferred_element_type=jnp.float32) + fc_bias_all[0].astype(
        jnp.float32
    )
    fired = gelu_tanh(pre).astype(jnp.bfloat16)
    branch_two = lax.psum(
        jnp.dot(fired, out_all, preferred_element_type=jnp.float32).astype(jnp.bfloat16), "mp"
    ).astype(jnp.float32)
    output = (hidden_one + branch_two + out_bias_all.astype(jnp.float32)).astype(jnp.bfloat16)
    grad_out = out_grad.astype(jnp.float32)
    out_bias_grad = jnp.sum(out_grad, axis=0, dtype=jnp.float32)
    out_weight_grad = jnp.einsum("tf,td->fd", fired, out_grad, preferred_element_type=jnp.float32)
    fired_grad = jnp.einsum("td,fd->tf", out_grad, out_all, preferred_element_type=jnp.float32)
    pre_grad = (fired_grad * gelu_slope(pre)).astype(jnp.bfloat16)
    fc_bias_grad = jnp.sum(pre_grad, axis=0, dtype=jnp.float32)
    fc_weight_grad = jnp.einsum("td,tf->df", act_two, pre_grad, preferred_element_type=jnp.float32)
    act_two_grad = lax.psum(
        jnp.einsum("tf,df->td", pre_grad, fc_all, preferred_element_type=jnp.float32).astype(
            jnp.bfloat16
        ),
        "mp",
    ).astype(jnp.float32)
    gain_two_grad = jnp.sum(act_two_grad * normed_two, axis=0)
    shift_two_grad = jnp.sum(act_two_grad, axis=0)
    hidden_grad = grad_out + norm_back(act_two_grad, gain_two_f, normed_two, inverse_two)
    branch_grad = hidden_grad.astype(jnp.bfloat16)
    proj_bias_grad = jnp.sum(branch_grad, axis=0, dtype=jnp.float32)
    proj_weight_grad = jnp.einsum(
        "te,td->ed", flat_rows, branch_grad, preferred_element_type=jnp.float32
    )
    rows_grad = (
        jnp.einsum("td,ed->te", branch_grad, proj_all, preferred_element_type=jnp.float32)
        .astype(jnp.bfloat16)
        .reshape(count, heads, HD)
    )
    query_grad, keys_grad, values_grad = attend_backward(
        query, keys, values, seg, log_sums, rows_grad
    )
    stacked = jnp.stack([query_grad, keys_grad, values_grad]).reshape(3, count, width)
    qkv_grad = jnp.einsum("td,cte->cde", act_one, stacked, preferred_element_type=jnp.float32)
    bias_sums = jnp.sum(stacked, axis=1, dtype=jnp.float32)
    qv_grad = jnp.stack([bias_sums[0], bias_sums[2]])[:, None, :]
    act_one_grad = lax.psum(
        jnp.einsum("cte,cde->td", stacked, qkv_all, preferred_element_type=jnp.float32).astype(
            jnp.bfloat16
        ),
        "mp",
    ).astype(jnp.float32)
    gain_one_grad = jnp.sum(act_one_grad * normed_one, axis=0)
    shift_one_grad = jnp.sum(act_one_grad, axis=0)
    input_grad = (
        hidden_grad + norm_back(act_one_grad, gain_one_f, normed_one, inverse_one)
    ).astype(jnp.bfloat16)
    mlp_grads = (
        lax.psum_scatter(gain_two_grad, "dp", scatter_dimension=0, tiled=True),
        lax.psum_scatter(shift_two_grad, "dp", scatter_dimension=0, tiled=True),
        lax.psum_scatter(fc_weight_grad, "dp", scatter_dimension=0, tiled=True),
        lax.psum_scatter(fc_bias_grad[None], "dp", scatter_dimension=1, tiled=True),
        lax.psum_scatter(out_weight_grad, "dp", scatter_dimension=1, tiled=True),
        lax.psum_scatter(out_bias_grad, "dp", scatter_dimension=0, tiled=True),
    )
    attn_grads = (
        summed_on_arrival(gain_one_grad.astype(jnp.bfloat16), "dp", 0),
        summed_on_arrival(shift_one_grad.astype(jnp.bfloat16), "dp", 0),
        summed_on_arrival(qkv_grad.astype(jnp.bfloat16), "dp", 1),
        summed_on_arrival(qv_grad.astype(jnp.bfloat16), "dp", 2),
        summed_on_arrival(proj_weight_grad.astype(jnp.bfloat16), "dp", 1),
        summed_on_arrival(proj_bias_grad.astype(jnp.bfloat16), "dp", 0),
    )
    return (
        output,
        input_grad,
        attn_grads[0],
        attn_grads[1],
        attn_grads[2],
        attn_grads[3],
        attn_grads[4],
        attn_grads[5],
        mlp_grads[0],
        mlp_grads[1],
        mlp_grads[2],
        mlp_grads[3],
        mlp_grads[4],
        mlp_grads[5],
    )


def solution(mesh):
    placed = (
        P("dp", None),
        P("dp", None),
        P("dp"),
        P("dp"),
        P(None, "dp", "mp"),
        P(None, "mp", "dp"),
        P("mp", "dp"),
        P("dp"),
        P("dp"),
        P("dp"),
        P("dp", "mp"),
        P("mp", "dp"),
        P("mp", "dp"),
        P("dp"),
        P("dp", None),
    )
    return jax.shard_map(
        per_device,
        mesh=mesh,
        in_specs=placed,
        out_specs=(
            P("dp", None),
            P("dp", None),
            P("dp"),
            P("dp"),
            P(None, "dp", "mp"),
            P(None, "mp", "dp"),
            P("mp", "dp"),
            P("dp"),
            P("dp"),
            P("dp"),
            P("dp", "mp"),
            P("mp", "dp"),
            P("mp", "dp"),
            P("dp"),
        ),
        check_vma=False,
    )
```

profile of v0, /device:TPU:0, one launch (start us, length us, event | category | flops | bytes accessed | tf_op | source)
XLA Modules:
  0.0 874.6 jit_solution(13929908678112195484)
XLA Ops:
  16.1 26.1 %all-reduce.14 = (bf16[768]{0:T(1024)(128)(2,1)}, bf16[768]{0:T(1024)(128)(2,1)}, bf16[768]{0:T(1024)(128)(2,1)}, bf16[768]{0:T(1024)(128)(2,1)S(1)}, bf16[768]{...) all-reduce(bf16[768]{0:T(1024)(128)(2,1)S(1)} %dynamic-update-slice, ...), channel_id=1, replica_groups=mesh['dp'=8,'mp'=4] {'dp'}, use_global_device_ids=true, to_apply=%add.7 | all-reduce | flops 5376 | bytes 21504
  47.7 13.0 %all_gather.38 = bf16[3,768,192]{2,0,1:T(4,128)(2,1)} all-gather(bf16[3,96,192]{2,0,1:T(4,128)(2,1)S(1)} %copy.90), channel_id=1, replica_groups=mesh['dp'=8,'mp'=4] {'dp'}, dimensions={1}, use_global_device_ids=true | all-gather | bytes 995328 | tf_op jit(solution)/shard_map/all_gather | solution.py:173
  72.4 8.2 all_gather.39
  82.5 9.8 %all_gather.40 = bf16[192,768]{0,1:T(8,128)(2,1)S(1)} all-gather(bf16[192,96]{0,1:T(8,128)(2,1)} %copy.95), channel_id=1, replica_groups=mesh['dp'=8,'mp'=4] {'dp'}, dimensions={1}, use_global_device_ids=true | all-gather | bytes 331776 | tf_op jit(solution)/shard_map/all_gather | solution.py:175
  100.4 53.0 %while.30 = (s32[]{:T(128)}, bf16[4,512,3,64]{1,3,2,0:T(8,128)(2,1)}, f32[4,3,512]{2,1,0:T(4,128)}, s32[4]{0:T(128)S(1)}, bf16[3072,3,64]{0,2,1:T(8,128)(2,1)}, ...) while((s32[]{:T(128)}, ...), condition=%wide.region_7.8_spmd, body=%wide.region_4.7_spmd.sunk | while | flops 634749440 | bytes 37845300 | solution.py:96
  164.5 116.1 %all-reduce.20.cloned.1.call-done = bf16[2048,768]{1,0:T(8,128)(2,1)} async-done(((bf16[2048,768]{1,0:T(8,128)(2,1)}), bf16[2048,768]{1,0:T(8,128)(2,1)}) %all-reduce.20.cloned.1.call-update) | async-done | bytes 3145744 | tf_op jit(solution)/shard_map/psum | solution.py:208
  289.2 9.8 %multiply_convert_fusion.1 = (bf16[2048,768]{1,0:T(8,128)(2,1)}, f32[2048,768]{1,0:T(8,128)}) fusion(f32[768]{0:T(1024)} %add.315, bf16[2048,768]{1,0:T(8,128)(2,1)} %add_convert_fusion.1, bf16[768,768]{1,0:T(8,128)(2,1)} %all-gather.3.cloned.1.call-done), kind=kOutput, calls=%fused_computation.99 | convolution fusion | flops 2431647744 | bytes 13765632 | tf_op jit(solution)/shard_map/dot_general | solution.py:214
  298.9 9.0 %convert_reduce_fusion.3 = (f32[768]{0:T(1024)}, bf16[2048,768]{1,0:T(8,128)(2,1)S(1)}) fusion(f32[2048,768]{1,0:T(8,128)} %get-tuple-element.446, f32[768]{0:T(1024)} %add.315, bf16[2048,768]{1,0:T(8,128)(2,1)} %param.33, bf16[768,768]{0,1:T(8,128)(2,1)} %all-gather.5.cloned.1.call-done), kind=kOutput, calls=%fused_computation.97 | convolution fusion | flops 2450521344 | bytes 13768704 | tf_op jit(solution)/shard_map/td,fd->tf/dot_general | solution.py:225
  321.8 112.0 %all-reduce.22.cloned.1.call-done = bf16[2048,768]{1,0:T(8,128)(2,1)} async-done(((bf16[2048,768]{1,0:T(8,128)(2,1)}), bf16[2048,768]{1,0:T(8,128)(2,1)}) %all-reduce.22.cloned.1.call-update) | async-done | bytes 3145744 | tf_op jit(solution)/shard_map/psum | solution.py:229
  433.9 7.2 fusion.73
  453.5 144.5 %while.31 = (s32[]{:T(128)}, f32[3072,3,64]{0,2,1:T(8,128)}, f32[3072,3,64]{0,2,1:T(8,128)}, bf16[4,512,3,64]{1,3,2,0:T(8,128)(2,1)}, s32[4]{0:T(128)S(1)}, /*in...) while((s32[]{:T(128)}, f32[3072,3,64]{0,2,1:T(8,128)}, ...), condition=%wide.region_17.18_spmd, body=%wide.region_15.17_spmd.sunk | while | flops 1534525952 | bytes 171319888 | solution.py:140
  461.7 7.2 multiply_reduce_fusion.3
  468.9 9.4 %multiply_convert_fusion.3 = bf16[3,512,1536]{2,1,0:T(8,128)(2,1)} fusion(f32[3,512,1536]{2,1,0:T(8,128)} %get-tuple-element.585, f32[3,512,1536]{2,1,0:T(8,128)} %copy-done, f32[3,512]{1,0:T(4,128)S(1)} %get-tuple-element.586), kind=kLoop, calls=%fused_computation.21.clone.1 | loop fusion | flops 7077888 | bytes 23599104 | tf_op jit(solution)/shard_map/while/body/eval_jaxpr/convert_element_type | solution.py:117
  497.7 7.2 multiply_reduce_fusion.3
  504.9 9.4 %multiply_convert_fusion.3 = bf16[3,512,1536]{2,1,0:T(8,128)(2,1)} fusion(f32[3,512,1536]{2,1,0:T(8,128)} %get-tuple-element.585, f32[3,512,1536]{2,1,0:T(8,128)} %copy-done, f32[3,512]{1,0:T(4,128)S(1)} %get-tuple-element.586), kind=kLoop, calls=%fused_computation.21.clone.1 | loop fusion | flops 7077888 | bytes 23599104 | tf_op jit(solution)/shard_map/while/body/eval_jaxpr/convert_element_type | solution.py:117
  533.9 7.2 multiply_reduce_fusion.3
  541.1 9.4 %multiply_convert_fusion.3 = bf16[3,512,1536]{2,1,0:T(8,128)(2,1)} fusion(f32[3,512,1536]{2,1,0:T(8,128)} %get-tuple-element.585, f32[3,512,1536]{2,1,0:T(8,128)} %copy-done, f32[3,512]{1,0:T(4,128)S(1)} %get-tuple-element.586), kind=kLoop, calls=%fused_computation.21.clone.1 | loop fusion | flops 7077888 | bytes 23599104 | tf_op jit(solution)/shard_map/while/body/eval_jaxpr/convert_element_type | solution.py:117
  570.0 7.2 multiply_reduce_fusion.3
  577.2 9.4 %multiply_convert_fusion.3 = bf16[3,512,1536]{2,1,0:T(8,128)(2,1)} fusion(f32[3,512,1536]{2,1,0:T(8,128)} %get-tuple-element.585, f32[3,512,1536]{2,1,0:T(8,128)} %copy-done, f32[3,512]{1,0:T(4,128)S(1)} %get-tuple-element.586), kind=kLoop, calls=%fused_computation.21.clone.1 | loop fusion | flops 7077888 | bytes 23599104 | tf_op jit(solution)/shard_map/while/body/eval_jaxpr/convert_element_type | solution.py:117
  613.7 6.9 fusion.93
  627.2 7.3 fusion.94
  672.2 29.2 %all-reduce.13 = (f32[768]{0:T(1024)}, f32[768]{0:T(1024)}, f32[768]{0:T(1024)}) all-reduce(f32[768]{0:T(1024)} %get-tuple-element.368, f32[768]{0:T(1024)} %get-tuple-element.374, f32[768]{0:T(1024)} %convert_reduce_fusion.2), channel_id=2, replica_groups=mesh['dp'=8,'mp'=4] {'dp'}, use_global_device_ids=true, to_apply=%region_32.33.clone | all-reduce | flops 2304 | bytes 18432
  710.8 125.2 %all-reduce.24.cloned.1.call-done = (bf16[2048,768]{1,0:T(8,128)(2,1)}, bf16[2048,768]{1,0:T(8,128)(2,1)}) async-done(((bf16[2048,768]{1,0:T(8,128)(2,1)}, bf16[2048,768]{1,0:T(8,128)(2,1)}), (bf16[2048,768]{1,0:T(8,128)(2,1)}, bf16[2048,768]{1,0:T(8,128)(2,1)})) %all-reduce.24.cloned.1.call-update) | async-done | bytes 6291472 | tf_op jit(solution)/shard_map/psum | solution.py:218
  847.6 9.2 %fusion.58 = (bf16[2048,768]{1,0:T(8,128)(2,1)}, bf16[2048,768]{1,0:T(8,128)(2,1)}) fusion(f32[2048,768]{1,0:T(8,128)} %copy-done.6, bf16[2048,768]{1,0:T(8,128)(2,1)S(1)} %copy-done.2, bf16[2048,768]{1,0:T(8,128)(2,1)S(1)} %copy-done.11, f32[2048]{0:T(1024)S(1)} %broadcast_multiply_fusion, f32[2048]{0:T(1024)S(1)} %broadcast_multiply_fusion.1, ...), kind=kLoop, calls=%fused_computation.80 | loop fusion | flops 28311552 | bytes 25207808 | tf_op jit(solution)/shard_map/convert_element_type | solution.py:265
  (367 shorter events, 288.0 us)
Async XLA Ops:
  8.0 56.2 %copy-start.2 = (bf16[2048,768]{1,0:T(8,128)(2,1)S(1)}, bf16[2048,768]{1,0:T(8,128)(2,1)}, u32[]{:S(2)}) copy-start(bf16[2048,768]{1,0:T(8,128)(2,1)} %param.19) | copy-start | bytes 9437188
  8.0 39.5 %copy-start.24 = (bf16[3,96,192]{2,1,0:T(8,128)(2,1)S(1)}, bf16[3,96,192]{2,1,0:T(8,128)(2,1)}, u32[]{:S(2)}) copy-start(bf16[3,96,192]{2,1,0:T(8,128)(2,1)} %param.23) | copy-start | bytes 331780
  8.0 272.6 %all-reduce.20.cloned.1.call-start = ((), (), s32[]{:S(2)}) async-start(), calls=%async_computation.9 | async-start | bytes 6291456 | tf_op jit(solution)/shard_map/psum | solution.py:208
  42.2 25.4 %copy-start.34 = (f32[768]{0:T(1024)}, f32[768]{0:T(1024)S(1)}, u32[]{:S(2)}) copy-start(f32[768]{0:T(1024)S(1)} %convert_element_type.218) | copy-start | bytes 9220
  42.2 25.4 %copy-start.41 = (f32[768]{0:T(1024)}, f32[768]{0:T(1024)S(1)}, u32[]{:S(2)}) copy-start(f32[768]{0:T(1024)S(1)} %convert_element_type.219) | copy-start | bytes 9220
  44.6 23.0 %copy-start.25 = (f32[2048]{0:T(1024)}, f32[2048]{0:T(1024)S(1)}, u32[]{:S(2)}) copy-start(f32[2048]{0:T(1024)S(1)} %broadcast_multiply_fusion.5) | copy-start | bytes 24580
  47.5 20.1 %copy-start.29 = (f32[2048]{0:T(1024)}, f32[2048]{0:T(1024)S(1)}, u32[]{:S(2)}) copy-start(f32[2048]{0:T(1024)S(1)} %add_rsqrt_fusion.1) | copy-start | bytes 24580
  159.1 130.1 %all-gather.3.cloned.1.call-start = ((), (), s32[]{:S(2)}) async-start(), calls=%async_computation.10 | async-start | bytes 1327104 | tf_op jit(solution)/shard_map/all_gather | solution.py:201
  159.7 139.3 %all-gather.5.cloned.1.call-start = ((), (), s32[]{:S(2)}) async-start(), calls=%async_computation.11 | async-start | bytes 1327104 | tf_op jit(solution)/shard_map/all_gather | solution.py:203
  160.3 273.6 %all-reduce.22.cloned.1.call-start = ((), (), s32[]{:S(2)}) async-start(), calls=%async_computation.12 | async-start | bytes 6291456 | tf_op jit(solution)/shard_map/psum | solution.py:229
  162.0 279.1 %copy-start.22 = (f32[768]{0:T(1024)}, f32[768]{0:T(1024)S(1)}, u32[]{:S(2)}) copy-start(f32[768]{0:T(1024)S(1)} %convert_element_type.231) | copy-start | bytes 9220
  313.6 357.2 %reduce-scatter.10.cloned.1.call-start = ((), (), s32[]{:S(2)}) async-start(), calls=%async_computation.15 | async-start | bytes 442368
  315.3 520.7 %all-reduce.24.cloned.1.call-start = ((), (), s32[]{:S(2)}) async-start(), calls=%async_computation.16 | async-start | bytes 12582912 | tf_op jit(solution)/shard_map/psum | solution.py:218
  613.6 253.2 %reduce-scatter.6.cloned.1.call-start = ((), (), s32[]{:S(2)}) async-start(), calls=%async_computation.13 | async-start | bytes 2654208 | tf_op jit(solution)/shard_map/reduce_scatter | solution.py:269
  623.4 11.7 %all-to-all-start.3 = ((bf16[8,2,1,24]{3,1,2,0:T(2,128)(2,1)}), bf16[8,2,1,24]{3,1,2,0:T(2,128)(2,1)S(1)}, u32[]{:S(2)}, u32[]{:S(2)}) async-start(bf16[8,2,1,24]{3,1,2,0:T(2,128)(2,1)} %copy.102), calls=%async_computation.3 | async-start | bytes 8192 | tf_op jit(solution)/shard_map/all_to_all | solution.py:24
  627.1 239.8 %reduce-scatter.8.cloned.1.call-start = ((), (), s32[]{:S(2)}) async-start(), calls=%async_computation.14 | async-start | bytes 2654208 | tf_op jit(solution)/shard_map/reduce_scatter | solution.py:271
  635.2 11.4 %all-to-all-start.5 = ((bf16[8,1,96]{2,1,0:T(2,128)(2,1)}), bf16[8,1,96]{2,1,0:T(2,128)(2,1)S(1)}, u32[]{:S(2)}, u32[]{:S(2)}) async-start(bf16[8,1,96]{2,1,0:T(2,128)(2,1)} %all_to_all.34), calls=%async_computation.5 | async-start | bytes 8192 | tf_op jit(solution)/shard_map/all_to_all | solution.py:24
  646.6 15.0 %all-to-all-start.4 = ((bf16[8,192,96]{2,1,0:T(8,128)(2,1)}), bf16[8,192,96]{2,1,0:T(8,128)(2,1)S(1)}, u32[]{:S(2)}, u32[]{:S(2)}) async-start(bf16[8,192,96]{2,1,0:T(8,128)(2,1)} %bitcast.99), calls=%async_computation.4 | async-start | bytes 786432 | tf_op jit(solution)/shard_map/all_to_all | solution.py:24
  661.6 46.8 %all-to-all-start.2 = ((bf16[8,3,96,192]{2,3,1,0:T(8,128)(2,1)}), bf16[8,3,96,192]{2,3,1,0:T(8,128)(2,1)}, u32[]{:S(2)}, u32[]{:S(2)}) async-start(bf16[8,3,96,192]{2,3,1,0:T(8,128)(2,1)} %bitcast.125), calls=%async_computation.2 | async-start | bytes 2359296 | tf_op jit(solution)/shard_map/all_to_all | solution.py:24
  670.8 176.8 %copy-start.23 = (f32[768]{0:T(1024)S(1)}, f32[768]{0:T(1024)}, u32[]{:S(2)}) copy-start(f32[768]{0:T(1024)} %copy-done.22) | copy-start | bytes 9220
  708.4 139.2 %copy-start.30 = (f32[2048]{0:T(1024)S(1)}, f32[2048]{0:T(1024)}, u32[]{:S(2)}) copy-start(f32[2048]{0:T(1024)} %copy-done.29) | copy-start | bytes 24580
  708.4 139.2 %copy-start.37 = (f32[768]{0:T(1024)S(1)}, f32[768]{0:T(1024)}, u32[]{:S(2)}) copy-start(f32[768]{0:T(1024)} %convert_element_type.238) | copy-start | bytes 9220
  839.1 18.4 %all-to-all-start.1 = ((bf16[8,1,96]{2,1,0:T(2,128)(2,1)}), bf16[8,1,96]{2,1,0:T(2,128)(2,1)S(1)}, u32[]{:S(2)}, u32[]{:S(2)}) async-start(bf16[8,1,96]{2,1,0:T(2,128)(2,1)} %all_to_all.33), calls=%async_computation.1 | async-start | bytes 8192 | tf_op jit(solution)/shard_map/all_to_all | solution.py:24
  857.5 8.8 %all-to-all-start = ((bf16[8,1,96]{2,1,0:T(2,128)(2,1)}), bf16[8,1,96]{2,1,0:T(2,128)(2,1)S(1)}, u32[]{:S(2)}, u32[]{:S(2)}) async-start(bf16[8,1,96]{2,1,0:T(2,128)(2,1)} %convert_element_type.266), calls=%async_computation | async-start | bytes 8192 | tf_op jit(solution)/shard_map/all_to_all | solution.py:24
  (64 other events, 331.6 us)
Sparse Core Ops, SparseCore 0:
  159.2 121.3 all-reduce.19
  313.7 120.0 all-reduce.21
  613.7 222.2 all-reduce.23
Sparse Core Ops, SparseCore 1:
  161.4 24.1 all-gather.2
  187.4 23.9 all-gather.4
  317.1 32.9 reduce-scatter.9
  620.7 42.3 reduce-scatter.5
  667.4 41.5 reduce-scatter.7
where the time goes:
time: 884 us; the launch traced here: 875 us
  waiting for transfers between devices  359 us (41%)
  matrix products  175 us (20%)
  other arithmetic  120 us (14%)
  blocking collectives  86.4 us (10%)
  local copies, waits for them, and re-layouts  78.7 us (9%)
  starting transfers between devices  25.1 us (3%)
  between operations  17.8 us (2%)
  loops' own time  13.5 us (2%)
    psum x1, waiting for transfers between devices, per_device(): lax.psum(jnp.dot(fired, out_all, preferred_element_type=jnp.float32).asty...  125 us
    psum x1, waiting for transfers between devices, per_device(): lax.psum(jnp.dot(flat_rows, proj_all, preferred_element_type=jnp.float32)...  116 us
    psum x1, waiting for transfers between devices, per_device(): lax.psum(jnp.einsum('tf,df->td', pre_grad, fc_all, preferred_element_type...  112 us
    unnamed x2, blocking collectives  55.3 us
    dot_general x8, matrix products, block_scores(): jnp.einsum('qhd,khd->hqk', q_rows, k_rows, preferred_element_type=jnp.flo...  41.6 us
    convert_element_type x4, other arithmetic, one_block(): score_grad = (probs * (prob_grad - jnp.sum(probs * prob_grad, axis=-1, ke...  37.6 us
    dot_general x4, matrix products, one_block(): jnp.einsum('hqk,qhd->khd', probs.astype(jnp.bfloat16), g_rows, preferred_...  24.7 us
    all_to_all x6, starting transfers between devices, summed_on_arrival(): pieces = lax.all_to_all(split_up(shard, dim, size), axis, 0, 0, tiled=True)  24.3 us
  transfers between devices with their start and end apart: 14, of which 4 were waited for; matrix products, arithmetic and copies ran while one was open for 29% of the time, Pallas kernels for 0%

commit v1 on v0

--- a/solution.py
+++ b/solution.py
@@ -1,17 +1,33 @@
+import functools
+
 import jax
 import jax.numpy as jnp
 from jax import lax
+from jax.experimental import pallas as pl
+from jax.experimental.pallas import tpu as pltpu
 from jax.sharding import PartitionSpec as P
 
 HD = 64
+HPD = 3
+WIDE = 256
 MAXLEN = 1024
-QBLOCK = 512
+QB = 256
+BAND = MAXLEN // QB
 
 
 EPS = 1e-05
 SCALE = 0.125
 NEG = -1e30
 GELU_C = 0.7978845608028654
+NN = (((1,), (0,)), ((), ()))
+NT = (((1,), (1,)), ((), ()))
+TN = (((0,), (0,)), ((), ()))
+f32 = jnp.float32
+bf16 = jnp.bfloat16
+
+
+def mm(left, right, dims=NN):
+    return lax.dot_general(left, right, dims, preferred_element_type=f32)
 
 
 def split_up(shard, dim, size):
@@ -53,99 +69,191 @@
     )
 
 
-def segment_ids(lengths_row, count):
+def segment_starts(lengths_row, count):
     ends = jnp.cumsum(lengths_row)
     places = jnp.arange(count, dtype=jnp.int32)
-    return jnp.sum((places[:, None] >= ends[None, :]).astype(jnp.int32), axis=1)
-
-
-def padded(array, span, fill):
-    front = jnp.full((span,) + array.shape[1:], fill, array.dtype)
-    return jnp.concatenate([front, array], axis=0)
-
-
-def block_scores(query, keys_pad, seg, seg_pad, index):
-    start = index * QBLOCK
-    q_rows = lax.dynamic_slice_in_dim(query, start, QBLOCK, 0)
-    k_rows = lax.dynamic_slice_in_dim(keys_pad, start, QBLOCK + MAXLEN, 0)
-    q_seg = lax.dynamic_slice_in_dim(seg, start, QBLOCK, 0)
-    k_seg = lax.dynamic_slice_in_dim(seg_pad, start, QBLOCK + MAXLEN, 0)
-    q_place = start + jnp.arange(QBLOCK, dtype=jnp.int32)
-    k_place = start - MAXLEN + jnp.arange(QBLOCK + MAXLEN, dtype=jnp.int32)
-    allowed = (q_seg[:, None] == k_seg[None, :]) & (k_place[None, :] <= q_place[:, None])
-    scores = jnp.einsum("qhd,khd->hqk", q_rows, k_rows, preferred_element_type=jnp.float32) * SCALE
-    return (jnp.where(allowed[None], scores, NEG), q_rows, k_rows)
-
-
-def attend_forward(query, keys, values, seg):
-    count, heads, size = query.shape
-    keys_pad = padded(keys, MAXLEN, 0)
-    values_pad = padded(values, MAXLEN, 0)
-    seg_pad = padded(seg, MAXLEN, -1)
-
-    def one_block(index):
-        masked, q_rows, k_rows = block_scores(query, keys_pad, seg, seg_pad, index)
-        v_rows = lax.dynamic_slice_in_dim(values_pad, index * QBLOCK, QBLOCK + MAXLEN, 0)
-        biggest = jnp.max(masked, axis=-1, keepdims=True)
-        expo = jnp.exp(masked - biggest)
-        total = jnp.sum(expo, axis=-1, keepdims=True)
-        probs = (expo / total).astype(jnp.bfloat16)
-        block_out = jnp.einsum("hqk,khd->qhd", probs, v_rows, preferred_element_type=jnp.float32)
-        return (block_out.astype(jnp.bfloat16), (biggest + jnp.log(total))[..., 0])
-
-    outs, log_sums = lax.map(one_block, jnp.arange(count // QBLOCK, dtype=jnp.int32))
-    return (outs.reshape(count, heads, size), log_sums)
-
-
-def attend_backward(query, keys, values, seg, log_sums, rows_grad):
-    count, heads, size = query.shape
-    keys_pad = padded(keys, MAXLEN, 0)
-    values_pad = padded(values, MAXLEN, 0)
-    seg_pad = padded(seg, MAXLEN, -1)
-    zeros = jnp.zeros((count + MAXLEN, heads, size), jnp.float32)
-
-    def one_block(carry, index):
-        key_acc, value_acc = carry
-        start = index * QBLOCK
-        masked, q_rows, k_rows = block_scores(query, keys_pad, seg, seg_pad, index)
-        v_rows = lax.dynamic_slice_in_dim(values_pad, start, QBLOCK + MAXLEN, 0)
-        g_rows = lax.dynamic_slice_in_dim(rows_grad, start, QBLOCK, 0)
-        probs = jnp.exp(masked - log_sums[index][:, :, None])
-        prob_grad = jnp.einsum("qhd,khd->hqk", g_rows, v_rows, preferred_element_type=jnp.float32)
-        score_grad = (
-            probs * (prob_grad - jnp.sum(probs * prob_grad, axis=-1, keepdims=True))
-        ).astype(jnp.bfloat16)
-        q_grad = (
-            jnp.einsum("hqk,khd->qhd", score_grad, k_rows, preferred_element_type=jnp.float32)
-            * SCALE
+    return jnp.max(jnp.where(ends[None, :] <= places[:, None], ends[None, :], 0), axis=1)[None, :]
+
+
+def rows_of(index, size=QB):
+    return pl.ds(pl.multiple_of(index * size, size), size)
+
+
+def tile_heads(x):
+    return jnp.concatenate([x] * HPD, axis=1)
+
+
+def allowed_keys(i, j, start_ref):
+    start = start_ref[:, rows_of(i)]
+    key = lax.broadcasted_iota(jnp.int32, (QB, QB), 0)
+    query = lax.broadcasted_iota(jnp.int32, (QB, QB), 1)
+    return (key >= start - j * QB) & (key <= query + (i - j) * QB)
+
+
+def stack_heads(x):
+    lane = lax.broadcasted_iota(jnp.int32, x.shape, 1)
+    return jnp.concatenate(
+        [
+            jnp.where((lane >= HD * h) & (lane < HD * h + HD), x, jnp.zeros_like(x))
+            for h in range(HPD)
+        ],
+        axis=0,
+    )
+
+
+def attend_block(i, q_ref, k_ref, vt_ref, start_ref, lse_ref, o_ref, qs, acc):
+    rows = rows_of(i)
+    qs[...] = stack_heads(q_ref[rows])
+    acc[...] = jnp.zeros_like(acc)
+
+    def step(jj, carry):
+        biggest, total = carry
+        j = i - jj
+        keys = rows_of(j)
+        s = mm(k_ref[keys], qs[...], NT)
+        s = jnp.where(tile_heads(allowed_keys(i, j, start_ref)), s, NEG)
+        new = jnp.maximum(biggest, jnp.max(s, axis=0, keepdims=True))
+        p = jnp.exp(s - new)
+        shrink = jnp.exp(biggest - new)
+        total = total * shrink + jnp.sum(p, axis=0, keepdims=True)
+        p = p.astype(bf16)
+        for h in range(HPD):
+            cols = slice(QB * h, QB * h + QB)
+            acc[:, cols] = acc[:, cols] * shrink[:, cols] + mm(
+                vt_ref[HD * h : HD * h + HD, keys], p[:, cols]
+            )
+        return new, total
+
+    biggest, total = lax.fori_loop(
+        0,
+        jnp.minimum(i, BAND) + 1,
+        step,
+        (jnp.full((1, HPD * QB), NEG, f32), jnp.zeros((1, HPD * QB), f32)),
+    )
+    lse_ref[i] = biggest + jnp.log(total)
+    inverse = 1.0 / total
+    out = jnp.concatenate(
+        [acc[:, QB * h : QB * h + QB] * inverse[:, QB * h : QB * h + QB] for h in range(HPD)]
+        + [jnp.zeros((WIDE - HPD * HD, QB), f32)],
+        axis=0,
+    )
+    o_ref[rows] = out.T.astype(bf16)
+
+
+def attend_block_back(i, grad, q_ref, k_ref, v_ref, kt_ref, o_ref, start_ref, lse_ref, dk, dv, qs, gs, dqt):
+    rows = rows_of(i)
+    qs[...] = stack_heads(q_ref[rows])
+    gs[...] = stack_heads(grad)
+    both = (grad.astype(f32) * o_ref[rows].astype(f32)).T
+    delta = jnp.concatenate(
+        [jnp.sum(both[HD * h : HD * h + HD], axis=0, keepdims=True) for h in range(HPD)], axis=1
+    )
+    lse = lse_ref[i]
+    dqt[...] = jnp.zeros_like(dqt)
+
+    def step(jj, _):
+        j = i - jj
+        keys = rows_of(j)
+        s = mm(k_ref[keys], qs[...], NT)
+        s = jnp.where(tile_heads(allowed_keys(i, j, start_ref)), s, NEG)
+        p = jnp.exp(s - lse)
+        dp = mm(v_ref[keys], gs[...], NT)
+        ds = (p * (dp - delta)).astype(bf16)
+        p = p.astype(bf16)
+        dv[keys] += mm(p, gs[...])
+        dk[keys] += mm(ds, qs[...])
+        for h in range(HPD):
+            dqt[HD * h : HD * h + HD] += mm(
+                kt_ref[HD * h : HD * h + HD, keys], ds[:, QB * h : QB * h + QB]
+            )
+        return 0
+
+    lax.fori_loop(0, jnp.minimum(i, BAND) + 1, step, 0)
+
+
+def forward_kernel(q_ref, k_ref, v_ref, start_ref, o_ref, lse_ref, vt, qs, acc):
+    blocks = q_ref.shape[0] // QB
+
+    def turn(i, _):
+        vt[:, rows_of(i)] = v_ref[rows_of(i)].T
+        return 0
+
+    lax.fori_loop(0, blocks, turn, 0)
+
+    def block(i, _):
+        attend_block(i, q_ref, k_ref, vt, start_ref, lse_ref, o_ref, qs, acc)
+        return 0
+
+    lax.fori_loop(0, blocks, block, 0)
+
+
+def backward_kernel(
+    q_ref, k_ref, v_ref, o_ref, g_ref, start_ref, lse_ref, d_ref, kt, qs, gs, dqt, dk, dv
+):
+    blocks = q_ref.shape[0] // QB
+
+    def turn(i, _):
+        kt[:, rows_of(i)] = k_ref[rows_of(i)].T
+        return 0
+
+    lax.fori_loop(0, blocks, turn, 0)
+    dk[...] = jnp.zeros_like(dk)
+    dv[...] = jnp.zeros_like(dv)
+
+    def block(turn_of, _):
+        i = blocks - 1 - turn_of
+        rows = rows_of(i)
+        attend_block_back(
+            i, g_ref[rows], q_ref, k_ref, v_ref, kt, o_ref, start_ref, lse_ref, dk, dv, qs, gs, dqt
         )
-        k_part = (
-            jnp.einsum("hqk,qhd->khd", score_grad, q_rows, preferred_element_type=jnp.float32)
-            * SCALE
-        )
-        v_part = jnp.einsum(
-            "hqk,qhd->khd", probs.astype(jnp.bfloat16), g_rows, preferred_element_type=jnp.float32
-        )
-        key_acc = lax.dynamic_update_slice_in_dim(
-            key_acc, lax.dynamic_slice_in_dim(key_acc, start, QBLOCK + MAXLEN, 0) + k_part, start, 0
-        )
-        value_acc = lax.dynamic_update_slice_in_dim(
-            value_acc,
-            lax.dynamic_slice_in_dim(value_acc, start, QBLOCK + MAXLEN, 0) + v_part,
-            start,
-            0,
-        )
-        return ((key_acc, value_acc), q_grad)
-
-    (key_acc, value_acc), q_blocks = lax.scan(
-        one_block, (zeros, zeros), jnp.arange(count // QBLOCK, dtype=jnp.int32)
-    )
-    query_grad = q_blocks.reshape(count, heads, size).astype(jnp.bfloat16)
-    return (
-        query_grad,
-        key_acc[MAXLEN:].astype(jnp.bfloat16),
-        value_acc[MAXLEN:].astype(jnp.bfloat16),
-    )
+        d_ref[0, rows] = (dqt[...].T * SCALE).astype(bf16)
+        d_ref[1, rows] = dk[rows].astype(bf16)
+        d_ref[2, rows] = dv[rows].astype(bf16)
+        return 0
+
+    lax.fori_loop(0, blocks, block, 0)
+
+
+VMEM = pl.BlockSpec(memory_space=pltpu.VMEM)
+LIMIT = pltpu.CompilerParams(vmem_limit_bytes=40 * 2**20)
+
+
+def attend_forward(query, keys, values, starts):
+    count = query.shape[0]
+    return pl.pallas_call(
+        forward_kernel,
+        out_shape=(
+            jax.ShapeDtypeStruct((count, WIDE), bf16),
+            jax.ShapeDtypeStruct((count // QB, 1, HPD * QB), f32),
+        ),
+        in_specs=[VMEM] * 4,
+        out_specs=(VMEM, VMEM),
+        scratch_shapes=[
+            pltpu.VMEM((WIDE, count), bf16),
+            pltpu.VMEM((HPD * QB, WIDE), bf16),
+            pltpu.VMEM((HD, HPD * QB), f32),
+        ],
+        compiler_params=LIMIT,
+    )(query, keys, values, starts)
+
+
+def attend_backward(query, keys, values, rows, grad, starts, lse):
+    count = query.shape[0]
+    return pl.pallas_call(
+        backward_kernel,
+        out_shape=jax.ShapeDtypeStruct((3, count, WIDE), bf16),
+        in_specs=[VMEM] * 7,
+        out_specs=VMEM,
+        scratch_shapes=[
+            pltpu.VMEM((WIDE, count), bf16),
+            pltpu.VMEM((HPD * QB, WIDE), bf16),
+            pltpu.VMEM((HPD * QB, WIDE), bf16),
+            pltpu.VMEM((WIDE, QB), f32),
+            pltpu.VMEM((count, WIDE), f32),
+            pltpu.VMEM((count, WIDE), f32),
+        ],
+        compiler_params=LIMIT,
+    )(query, keys, values, rows, grad, starts, lse)
 
 
 def per_device(
@@ -166,7 +274,7 @@
     out_grad,
 ):
     count = tokens.shape[0]
-    seg = segment_ids(lengths[0], count)
+    starts = segment_starts(lengths[0], count)
     gain_one, shift_one, qkv_all, qv_all, proj_all, proj_bias_all = (
         lax.all_gather(first_gain, "dp", axis=0, tiled=True),
         lax.all_gather(first_shift, "dp", axis=0, tiled=True),
@@ -181,20 +289,14 @@
     act_one = (normed_one * gain_one_f + shift_one.astype(jnp.float32)).astype(jnp.bfloat16)
     projected = jnp.einsum("td,cde->cte", act_one, qkv_all, preferred_element_type=jnp.float32)
     width = qkv_all.shape[2]
-    heads = width // HD
-    query = (
-        (projected[0] + qv_all[0, 0].astype(jnp.float32))
-        .astype(jnp.bfloat16)
-        .reshape(count, heads, HD)
-    )
-    keys = projected[1].astype(jnp.bfloat16).reshape(count, heads, HD)
-    values = (
-        (projected[2] + qv_all[1, 0].astype(jnp.float32))
-        .astype(jnp.bfloat16)
-        .reshape(count, heads, HD)
-    )
-    attn_rows, log_sums = attend_forward(query, keys, values, seg)
-    flat_rows = attn_rows.reshape(count, width)
+    wide = ((0, 0), (0, WIDE - width))
+    query = jnp.pad(
+        (projected[0] + qv_all[0, 0].astype(f32)).astype(bf16) * jnp.asarray(SCALE, bf16), wide
+    )
+    keys = jnp.pad(projected[1].astype(bf16), wide)
+    values = jnp.pad((projected[2] + qv_all[1, 0].astype(f32)).astype(bf16), wide)
+    wide_rows, lse = attend_forward(query, keys, values, starts)
+    flat_rows = wide_rows[:, :width]
     gain_two, shift_two, fc_all, fc_bias_all, out_all, out_bias_all = (
         lax.all_gather(second_gain, "dp", axis=0, tiled=True),
         lax.all_gather(second_shift, "dp", axis=0, tiled=True),
@@ -240,15 +342,12 @@
     proj_weight_grad = jnp.einsum(
         "te,td->ed", flat_rows, branch_grad, preferred_element_type=jnp.float32
     )
-    rows_grad = (
-        jnp.einsum("td,ed->te", branch_grad, proj_all, preferred_element_type=jnp.float32)
-        .astype(jnp.bfloat16)
-        .reshape(count, heads, HD)
-    )
-    query_grad, keys_grad, values_grad = attend_backward(
-        query, keys, values, seg, log_sums, rows_grad
-    )
-    stacked = jnp.stack([query_grad, keys_grad, values_grad]).reshape(3, count, width)
+    rows_grad = jnp.einsum(
+        "td,ed->te", branch_grad, proj_all, preferred_element_type=jnp.float32
+    ).astype(jnp.bfloat16)
+    stacked = attend_backward(
+        query, keys, values, wide_rows, jnp.pad(rows_grad, wide), starts, lse
+    )[:, :, :width]
     qkv_grad = jnp.einsum("td,cte->cde", act_one, stacked, preferred_element_type=jnp.float32)
     bias_sums = jnp.sum(stacked, axis=1, dtype=jnp.float32)
     qv_grad = jnp.stack([bias_sums[0], bias_sums[2]])[:, None, :]

time: 884 us -> 721 us (0.82)
  matrix products: 175 us -> 65.9 us
  other arithmetic: 120 us -> 56.1 us
  Pallas kernels: 0 us -> 44.5 us
  local copies, waits for them, and re-layouts: 78.7 us -> 51.6 us
  loops' own time: 13.5 us -> 0 us
    dot_general x28 -> x0, matrix products: 107 us -> none  [the longest x8 41.6 us: block_scores(): jnp.einsum('qhd,khd->hqk', q_rows, k_rows, preferred_element_type=jnp.flo...]
    pallas_call x0 -> x2, Pallas kernels: none -> 44.5 us  [the longest x1 24.6 us: attend_backward(): pl.pallas_call(backward_kernel, out_shape=jax.ShapeDtypeStruct((3, count,...]
    convert_element_type x7 -> x2, other arithmetic: 42.7 us -> 2.89 us  [the longest x1 1.76 us: per_device(): (projected[2] + qv_all[1, 0].astype(f32)).astype(bf16)]
    another operation x2 -> x0, loops' own time: 13.5 us -> none  [the longest x1 10.7 us: attend_backward(): lax.scan(one_block, (zeros, zeros), jnp.arange(count // QBLOCK, dtype=jnp...]
    reduce_sum x5 -> x0, other arithmetic: 12.1 us -> none  [the longest x4 11.4 us: one_block(): total = jnp.sum(expo, axis=-1, keepdims=True)]
    dynamic_slice x24 -> x0, local copies, waits for them, and re-layouts: 11.4 us -> none  [the longest x8 6.13 us: block_scores(): q_seg = lax.dynamic_slice_in_dim(seg, start, QBLOCK, 0)]
    unnamed x101 -> x86, local copies, waits for them, and re-layouts: 22.8 us -> 26.7 us
  transfers between devices with their start and end apart: 14 -> 14, of which waited for: 4 -> 4; matrix products, arithmetic and copies ran while one was open for 29% -> 15% of each run, Pallas kernels for 0% -> 3%
where the time goes in v1:
time: 721 us; the launch traced here: 711 us
  waiting for transfers between devices  362 us (50%)
  blocking collectives  88.1 us (12%)
  matrix products  65.9 us (9%)
  other arithmetic  56.1 us (8%)
  local copies, waits for them, and re-layouts  51.6 us (7%)
  Pallas kernels  44.5 us (6%)
  starting transfers between devices  25.5 us (4%)
  between operations  17.7 us (2%)
    psum x1, waiting for transfers between devices, per_device(): lax.psum(jnp.dot(fired, out_all, preferred_element_type=jnp.float32).asty...  125 us
    psum x1, waiting for transfers between devices, per_device(): lax.psum(jnp.dot(flat_rows, proj_all, preferred_element_type=jnp.float32)...  120 us
    psum x1, waiting for transfers between devices, per_device(): lax.psum(jnp.einsum('tf,df->td', pre_grad, fc_all, preferred_element_type...  113 us
    unnamed x2, blocking collectives  55.2 us
    unnamed x86, local copies, waits for them, and re-layouts  26.7 us
    pallas_call x1, Pallas kernels, attend_backward(): pl.pallas_call(backward_kernel, out_shape=jax.ShapeDtypeStruct((3, count,...  24.6 us
    all_to_all x6, starting transfers between devices, summed_on_arrival(): pieces = lax.all_to_all(split_up(shard, dim, size), axis, 0, 0, tiled=True)  24.3 us
    pallas_call x1, Pallas kernels, attend_forward(): pl.pallas_call(forward_kernel, out_shape=(jax.ShapeDtypeStruct((count, WI...  19.9 us
  transfers between devices with their start and end apart: 14, of which 4 were waited for; matrix products, arithmetic and copies ran while one was open for 15% of the time, Pallas kernels for 3%

profile of v1, /device:TPU:0, one launch (start us, length us, event | category | flops | bytes accessed | tf_op | source)
XLA Modules:
  0.0 711.5 jit_solution(9058821448379070419)
XLA Ops:
  16.0 26.0 %all-reduce.15 = (bf16[768]{0:T(1024)(128)(2,1)S(1)}, bf16[768]{0:T(1024)(128)(2,1)S(1)}, bf16[768]{0:T(1024)(128)(2,1)S(1)}, bf16[768]{0:T(1024)(128)(2,1)S(1)}...) all-reduce(bf16[768]{0:T(1024)(128)(2,1)S(1)} %dynamic-update-slice, ...), channel_id=1, replica_groups=mesh['dp'=8,'mp'=4] {'dp'}, use_global_device_ids=true, to_apply=%add.8 | all-reduce | flops 5376 | bytes 21504
  48.7 7.8 %all_gather.39 = bf16[2,1,192]{1,0,2:T(2,128)(2,1)S(1)} all-gather(bf16[2,1,24]{1,0,2:T(2,128)(2,1)S(1)} %copy.123), channel_id=1, replica_groups=mesh['dp'=8,'mp'=4] {'dp'}, dimensions={2}, use_global_device_ids=true | all-gather | bytes 864 | tf_op jit(solution)/shard_map/all_gather | solution.py:282
  57.7 11.0 %all_gather.40 = bf16[192,768]{0,1:T(8,128)(2,1)} all-gather(bf16[192,96]{0,1:T(8,128)(2,1)S(1)} %copy.125), channel_id=1, replica_groups=mesh['dp'=8,'mp'=4] {'dp'}, dimensions={1}, use_global_device_ids=true | all-gather | bytes 331776 | tf_op jit(solution)/shard_map/all_gather | solution.py:283
  68.8 14.1 %all_gather.38 = bf16[3,768,192]{2,0,1:T(4,128)(2,1)} all-gather(bf16[3,96,192]{2,0,1:T(4,128)(2,1)S(1)} %copy.120), channel_id=1, replica_groups=mesh['dp'=8,'mp'=4] {'dp'}, dimensions={1}, use_global_device_ids=true | all-gather | bytes 995328 | tf_op jit(solution)/shard_map/all_gather | solution.py:281
  86.3 5.2 fusion.59
  91.5 6.2 copy.122
  104.2 19.9 %shard_map.254 = (bf16[2048,256]{1,0:T(8,128)(2,1)S(1)}, f32[8,1,768]{2,1,0:T(1,128)S(1)}) custom-call(bf16[2048,256]{1,0:T(8,128)(2,1)S(1)} %pad.13.q_ref, bf16[2048,256]{1,0:T(8,128)(2,1)S(1)} %pad.14.k_ref, bf16[2048,256]{1,0:T(8,128)(2,1)S(1)} %pad.15.v_ref, s32[1,2048]{1,0:T(1,128)S(1)} %bitcast.69), custom_call_target="tpu_custom_call" | custom-call | tf_op jit(solution)/shard_map/pallas_call | solution.py:223
  129.5 119.8 %all-reduce.21.cloned.1.call-done = bf16[2048,768]{1,0:T(8,128)(2,1)} async-done(((bf16[2048,768]{1,0:T(8,128)(2,1)}), bf16[2048,768]{1,0:T(8,128)(2,1)}) %all-reduce.21.cloned.1.call-update) | async-done | bytes 3145744 | tf_op jit(solution)/shard_map/psum | solution.py:310
  257.2 9.7 %multiply_convert_fusion = (bf16[2048,768]{1,0:T(8,128)(2,1)}, f32[2048,768]{1,0:T(8,128)}) fusion(f32[768]{0:T(1024)S(1)} %add.172, bf16[2048,768]{1,0:T(8,128)(2,1)} %add_convert_fusion.1, bf16[768,768]{1,0:T(8,128)(2,1)} %all-gather.3.cloned.1.call-done), kind=kOutput, calls=%fused_computation.46 | convolution fusion | flops 2431647744 | bytes 13765632 | tf_op jit(solution)/shard_map/dot_general | solution.py:316
  267.0 8.4 %convert_reduce_fusion.3 = (f32[768]{0:T(1024)S(1)}, bf16[2048,768]{1,0:T(8,128)(2,1)S(1)}) fusion(f32[2048,768]{1,0:T(8,128)} %get-tuple-element.146, f32[768]{0:T(1024)S(1)} %add.172, bf16[2048,768]{1,0:T(8,128)(2,1)} %param.29, bf16[768,768]{0,1:T(8,128)(2,1)} %all-gather.5.cloned.1.call-done), kind=kOutput, calls=%fused_computation.44 | convolution fusion | flops 2450521344 | bytes 13768704 | tf_op jit(solution)/shard_map/td,fd->tf/dot_general | solution.py:327
  282.3 6.5 convolution_convert_fusion.1
  288.8 112.5 %all-reduce.23.cloned.1.call-done = bf16[2048,768]{1,0:T(8,128)(2,1)} async-done(((bf16[2048,768]{1,0:T(8,128)(2,1)}), bf16[2048,768]{1,0:T(8,128)(2,1)}) %all-reduce.23.cloned.1.call-update) | async-done | bytes 3145744 | tf_op jit(solution)/shard_map/psum | solution.py:331
  401.4 7.0 fusion.30
  421.7 24.6 %shard_map.255 = bf16[3,2048,256]{2,1,0:T(8,128)(2,1)S(1)} custom-call(bf16[2048,256]{1,0:T(8,128)(2,1)S(1)} %copy-done.5, bf16[2048,256]{1,0:T(8,128)(2,1)S(1)} %copy-done.3, bf16[2048,256]{1,0:T(8,128)(2,1)S(1)} %copy-done.1, bf16[2048,256]{1,0:T(8,128)(2,1)S(1)} %copy-done.7, bf16[2048,256]{1,0:T(8,128)(2,1)S(1)} %pad.16.g_ref, s32[1,2048]{1,0:T(1,128)S(1)} %bitcast.70, ...), custom_call_target="tpu_custom_call" | custom-call | tf_op jit(solution)/shard_map/pallas_call | solution.py:242
  450.7 7.0 fusion.62
  462.9 7.3 %fusion.63 = f32[768,768]{0,1:T(8,128)} fusion(bf16[2048,768]{1,0:T(8,128)(2,1)} %get-tuple-element.145, bf16[2048,768]{1,0:T(8,128)(2,1)} %param.29), kind=kOutput, calls=%fused_computation.106 | convolution fusion | flops 2415919104 | bytes 8650752 | tf_op jit(solution)/shard_map/tf,td->fd/dot_general | solution.py:326
  475.6 4.5 convolution_convert_fusion.4
  487.8 5.2 fusion.45
  498.9 4.5 all-to-all-start.2
  509.8 29.1 %all-reduce.14 = (f32[768]{0:T(1024)}, f32[768]{0:T(1024)}, f32[768]{0:T(1024)}) all-reduce(f32[768]{0:T(1024)} %get-tuple-element.116, f32[768]{0:T(1024)} %get-tuple-element.122, f32[768]{0:T(1024)} %convert_reduce_fusion.2), channel_id=2, replica_groups=mesh['dp'=8,'mp'=4] {'dp'}, use_global_device_ids=true, to_apply=%region_25.26.clone | all-reduce | flops 2304 | bytes 18432
  548.3 124.5 %all-reduce.25.cloned.1.call-done = (bf16[2048,768]{1,0:T(8,128)(2,1)}, bf16[2048,768]{1,0:T(8,128)(2,1)}) async-done(((bf16[2048,768]{1,0:T(8,128)(2,1)}, bf16[2048,768]{1,0:T(8,128)(2,1)}), (bf16[2048,768]{1,0:T(8,128)(2,1)}, bf16[2048,768]{1,0:T(8,128)(2,1)})) %all-reduce.25.cloned.1.call-update) | async-done | bytes 6291472 | tf_op jit(solution)/shard_map/psum | solution.py:320
  679.6 4.8 fusion.18
  684.4 9.2 %fusion.15 = (bf16[2048,768]{1,0:T(8,128)(2,1)}, bf16[2048,768]{1,0:T(8,128)(2,1)}) fusion(f32[2048,768]{1,0:T(8,128)} %copy-done.13, bf16[2048,768]{1,0:T(8,128)(2,1)S(1)} %copy-done.9, bf16[2048,768]{1,0:T(8,128)(2,1)S(1)} %copy-done.14, f32[2048]{0:T(1024)S(1)} %broadcast_multiply_fusion, f32[2048]{0:T(1024)S(1)} %broadcast_multiply_fusion.1, ...), kind=kLoop, calls=%fused_computation.27 | loop fusion | flops 28311552 | bytes 25207808 | tf_op jit(solution)/shard_map/convert_element_type | solution.py:364
  694.3 4.2 all-to-all-start
  (176 shorter events, 114.6 us)
Async XLA Ops:
  8.0 78.3 %copy-start.8 = (bf16[2048,768]{1,0:T(8,128)(2,1)S(1)}, bf16[2048,768]{1,0:T(8,128)(2,1)}, u32[]{:S(2)}) copy-start(bf16[2048,768]{1,0:T(8,128)(2,1)} %param.15) | copy-start | bytes 9437188
  8.0 40.4 %copy-start.28 = (bf16[2,1,24]{2,0,1:T(2,128)(2,1)S(1)}, bf16[2,1,24]{2,0,1:T(2,128)(2,1)}, u32[]{:S(2)}) copy-start(bf16[2,1,24]{2,0,1:T(2,128)(2,1)} %param.20) | copy-start | bytes 292
  8.0 40.6 %copy-start.23 = (bf16[192,96]{1,0:T(8,128)(2,1)S(1)}, bf16[192,96]{1,0:T(8,128)(2,1)}, u32[]{:S(2)}) copy-start(bf16[192,96]{1,0:T(8,128)(2,1)} %param.21) | copy-start | bytes 110596
  8.0 49.6 %copy-start.20 = (bf16[3,96,192]{2,1,0:T(8,128)(2,1)S(1)}, bf16[3,96,192]{2,1,0:T(8,128)(2,1)}, u32[]{:S(2)}) copy-start(bf16[3,96,192]{2,1,0:T(8,128)(2,1)} %param.19) | copy-start | bytes 331780
  8.1 241.3 %all-reduce.21.cloned.1.call-start = ((), (), s32[]{:S(2)}) async-start(), calls=%async_computation.9 | async-start | bytes 6291456 | tf_op jit(solution)/shard_map/psum | solution.py:310
  42.1 49.4 %copy-start.27 = (f32[768]{0:T(1024)}, f32[768]{0:T(1024)S(1)}, u32[]{:S(2)}) copy-start(f32[768]{0:T(1024)S(1)} %convert_element_type.175) | copy-start | bytes 9220
  48.5 43.0 %copy-start.21 = (f32[2048]{0:T(1024)}, f32[2048]{0:T(1024)S(1)}, u32[]{:S(2)}) copy-start(f32[2048]{0:T(1024)S(1)} %add_rsqrt_fusion.1) | copy-start | bytes 24580
  127.8 129.4 %all-gather.3.cloned.1.call-start = ((), (), s32[]{:S(2)}) async-start(), calls=%async_computation.10 | async-start | bytes 1327104 | tf_op jit(solution)/shard_map/all_gather | solution.py:303
  128.4 138.6 %all-gather.5.cloned.1.call-start = ((), (), s32[]{:S(2)}) async-start(), calls=%async_computation.11 | async-start | bytes 1327104 | tf_op jit(solution)/shard_map/all_gather | solution.py:305
  129.0 272.4 %all-reduce.23.cloned.1.call-start = ((), (), s32[]{:S(2)}) async-start(), calls=%async_computation.12 | async-start | bytes 6291456 | tf_op jit(solution)/shard_map/psum | solution.py:331
  281.1 227.3 %reduce-scatter.10.cloned.1.call-start = ((), (), s32[]{:S(2)}) async-start(), calls=%async_computation.15 | async-start | bytes 442368
  282.1 390.7 %all-reduce.25.cloned.1.call-start = ((), (), s32[]{:S(2)}) async-start(), calls=%async_computation.16 | async-start | bytes 12582912 | tf_op jit(solution)/shard_map/psum | solution.py:320
  416.5 29.8 %copy-start.19 = (bf16[3,768,192]{1,2,0:T(8,128)(2,1)S(1)}, bf16[3,768,192]{1,2,0:T(8,128)(2,1)}, u32[]{:S(2)}) copy-start(bf16[3,768,192]{1,2,0:T(8,128)(2,1)} %copy.121) | copy-start | bytes 2654212
  450.4 253.3 %reduce-scatter.6.cloned.1.call-start = ((), (), s32[]{:S(2)}) async-start(), calls=%async_computation.13 | async-start | bytes 2654208 | tf_op jit(solution)/shard_map/reduce_scatter | solution.py:368
  459.2 11.7 %all-to-all-start.3 = ((bf16[8,2,1,24]{3,1,2,0:T(2,128)(2,1)}), bf16[8,2,1,24]{3,1,2,0:T(2,128)(2,1)S(1)}, u32[]{:S(2)}, u32[]{:S(2)}) async-start(bf16[8,2,1,24]{3,1,2,0:T(2,128)(2,1)} %copy.134), calls=%async_computation.3 | async-start | bytes 8192 | tf_op jit(solution)/shard_map/all_to_all | solution.py:40
  462.8 240.9 %reduce-scatter.8.cloned.1.call-start = ((), (), s32[]{:S(2)}) async-start(), calls=%async_computation.14 | async-start | bytes 2654208 | tf_op jit(solution)/shard_map/reduce_scatter | solution.py:370
  471.5 11.6 %all-to-all-start.5 = ((bf16[8,1,96]{2,1,0:T(2,128)(2,1)}), bf16[8,1,96]{2,1,0:T(2,128)(2,1)S(1)}, u32[]{:S(2)}, u32[]{:S(2)}) async-start(bf16[8,1,96]{2,1,0:T(2,128)(2,1)} %all_to_all.34), calls=%async_computation.5 | async-start | bytes 8192 | tf_op jit(solution)/shard_map/all_to_all | solution.py:40
  483.7 15.3 %all-to-all-start.4 = ((bf16[8,192,96]{2,1,0:T(8,128)(2,1)}), bf16[8,192,96]{2,1,0:T(8,128)(2,1)S(1)}, u32[]{:S(2)}, u32[]{:S(2)}) async-start(bf16[8,192,96]{2,1,0:T(8,128)(2,1)} %bitcast.68), calls=%async_computation.4 | async-start | bytes 786432 | tf_op jit(solution)/shard_map/all_to_all | solution.py:40
  496.2 183.3 %copy-start.9 = (bf16[2048,768]{1,0:T(8,128)(2,1)S(1)}, bf16[2048,768]{1,0:T(8,128)(2,1)}, u32[]{:S(2)}) copy-start(bf16[2048,768]{1,0:T(8,128)(2,1)} %param.15) | copy-start | bytes 9437188
  498.9 47.0 %all-to-all-start.2 = ((bf16[8,3,96,192]{2,3,1,0:T(8,128)(2,1)}), bf16[8,3,96,192]{2,3,1,0:T(8,128)(2,1)}, u32[]{:S(2)}, u32[]{:S(2)}) async-start(bf16[8,3,96,192]{2,3,1,0:T(8,128)(2,1)} %bitcast.74), calls=%async_computation.2 | async-start | bytes 2359296 | tf_op jit(solution)/shard_map/all_to_all | solution.py:40
  545.9 138.5 %copy-start.22 = (f32[2048]{0:T(1024)S(1)}, f32[2048]{0:T(1024)}, u32[]{:S(2)}) copy-start(f32[2048]{0:T(1024)} %copy-done.21) | copy-start | bytes 24580
  545.9 138.5 %copy-start.24 = (f32[768]{0:T(1024)S(1)}, f32[768]{0:T(1024)}, u32[]{:S(2)}) copy-start(f32[768]{0:T(1024)} %convert_element_type.193) | copy-start | bytes 9220
  675.9 18.4 %all-to-all-start.1 = ((bf16[8,1,96]{2,1,0:T(2,128)(2,1)}), bf16[8,1,96]{2,1,0:T(2,128)(2,1)S(1)}, u32[]{:S(2)}, u32[]{:S(2)}) async-start(bf16[8,1,96]{2,1,0:T(2,128)(2,1)} %all_to_all.33), calls=%async_computation.1 | async-start | bytes 8192 | tf_op jit(solution)/shard_map/all_to_all | solution.py:40
  694.3 8.8 %all-to-all-start = ((bf16[8,1,96]{2,1,0:T(2,128)(2,1)}), bf16[8,1,96]{2,1,0:T(2,128)(2,1)S(1)}, u32[]{:S(2)}, u32[]{:S(2)}) async-start(bf16[8,1,96]{2,1,0:T(2,128)(2,1)} %convert_element_type.219), calls=%async_computation | async-start | bytes 8192 | tf_op jit(solution)/shard_map/all_to_all | solution.py:40
  (21 other events, 127.0 us)
Sparse Core Ops, SparseCore 0:
  127.9 121.3 all-reduce.20
  281.2 120.0 all-reduce.22
  450.5 222.2 all-reduce.24
Sparse Core Ops, SparseCore 1:
  130.2 24.1 all-gather.2
  156.1 23.9 all-gather.4
  284.6 32.9 reduce-scatter.9
  457.8 42.2 reduce-scatter.5
  504.3 41.6 reduce-scatter.7

commit v2 on v1

--- a/solution.py
+++ b/solution.py
@@ -396,6 +396,722 @@
     )
 
 
+MESH = pl.DeviceIdType.MESH
+TB = 512
+RB = 128
+
+
+def norm(values):
+    mean = jnp.mean(values, axis=-1, keepdims=True)
+    centred = values - mean
+    inverse = lax.rsqrt(jnp.mean(centred * centred, axis=-1, keepdims=True) + EPS)
+    return centred * inverse, inverse
+
+
+def remote(src, dst, send, recv, device):
+    return pltpu.make_async_remote_copy(
+        src_ref=src, dst_ref=dst, send_sem=send, recv_sem=recv, device_id=device, device_id_type=MESH
+    )
+
+
+def whole_kernel(
+    tokens,
+    grads,
+    starts,
+    fc_own,
+    out_own,
+    qkv_own,
+    par_own,
+    output,
+    grad_tokens,
+    dw_out,
+    dwp_out,
+    pg_out,
+    w_fc,
+    w_out,
+    w_qkv,
+    pars,
+    par,
+    fcb,
+    qr,
+    kr,
+    vr,
+    turned,
+    orow,
+    rows_all,
+    lse,
+    qs,
+    gs,
+    acc,
+    dqt,
+    dk,
+    dv,
+    gbuf,
+    normed,
+    inv,
+    act,
+    oacc,
+    gacc,
+    fired,
+    preg,
+    rowg,
+    stacked,
+    hid,
+    dw,
+    dwp,
+    pgrad,
+    pgbuf,
+    part,
+    edge,
+    far,
+    q_s,
+    q_r,
+    p_s,
+    p_r,
+    z_s,
+    z_r,
+    w_s,
+    w_r,
+    a_s,
+    a_r,
+    ar_s,
+    ar_r,
+    d_s,
+    d_r,
+    g_s,
+    g_r,
+    loc,
+    free,
+):
+    d = lax.axis_index("dp")
+    m = lax.axis_index("mp")
+    y, x, k = d // 4, (d // 2) % 2, d % 2
+    count = tokens.shape[0]
+    blocks, subs = count // TB, count // QB
+
+    def place(yy, xx, kk):
+        return (yy * 4 + xx * 2 + kk, m)
+
+    flat_fc = w_fc.reshape(4, 768, 1024)
+    flat_out = w_out.reshape(4, 768, 768)
+    flat_qkv = w_qkv.reshape(768, 3 * WIDE)
+    x_dev, y_dev, diag, twin = (
+        place(y, 1 - x, k),
+        place(1 - y, x, k),
+        place(1 - y, 1 - x, k),
+        place(y, x, 1 - k),
+    )
+    plane = [(lax.rem(d + o, 8), m) for o in range(8)]
+    line = [(d, lax.rem(m + o, 4)) for o in range(4)]
+    came = [lax.rem(m + 4 - o, 4) for o in range(4)]
+
+    barrier = pltpu.get_barrier_semaphore()
+    for device in plane[1:] + line[1:]:
+        pl.semaphore_signal(barrier, inc=1, device_id=device, device_id_type=MESH)
+    pl.semaphore_wait(barrier, 10)
+
+    q_send = [
+        remote(qkv_own, w_qkv.at[y, x, k], q_s.at[i], q_r.at[i], device)
+        for i, device in enumerate((x_dev, y_dev, diag, twin))
+    ]
+    q_from = [(y, 1 - x, k), (1 - y, x, k), (1 - y, 1 - x, k)]
+    q_pass = [
+        remote(w_qkv.at[c], w_qkv.at[c], q_s.at[4 + i], q_r.at[4 + i], twin)
+        for i, c in enumerate(q_from)
+    ]
+    for copy in q_send:
+        copy.start()
+    p_send = [remote(par_own, pars.at[o], p_s.at[o], p_r.at[o], plane[o]) for o in range(1, 8)]
+    for copy in p_send:
+        copy.start()
+    own = (fc_own, out_own)
+    held = (w_fc, w_out)
+    z_send = [
+        [
+            remote(own[c], held[c].at[m, y, x, k], z_s.at[c, o], z_r.at[c, o], line[o])
+            for o in range(1, 4)
+        ]
+        for c in range(2)
+    ]
+    for o in range(3):
+        for c in range(2):
+            z_send[c][o].start()
+    w_fc[m, y, x, k] = fc_own[...]
+    w_out[m, y, x, k] = out_own[...]
+    w_qkv[y, x, k] = qkv_own[...]
+    pars[0] = par_own[...]
+
+    def hop(o, c, stage):
+        s = came[o]
+        if stage == 0:
+            part_of = held[c].at[s, y, x, k]
+            device = (x_dev, y_dev)[c]
+        elif stage == 1:
+            part_of = (held[0].at[s, y, :, k], held[1].at[s, :, x, k])[c]
+            device = (y_dev, x_dev)[c]
+        else:
+            part_of = held[c].at[s, :, :, k]
+            device = twin
+        return remote(part_of, part_of, w_s.at[c, stage, o], w_r.at[c, stage, o], device)
+
+    def advance(o, stage):
+        for c in range(2):
+            if stage > 0:
+                hop(o, c, stage - 1).wait_recv()
+            elif o > 0:
+                z_send[c][o - 1].wait_recv()
+            hop(o, c, stage).start()
+
+    advance(0, 0)
+    g_in = [
+        pltpu.make_async_copy(
+            grads.at[pl.ds((blocks - 1 - t) * TB, TB)], gbuf.at[t % 2], loc.at[t % 2]
+        )
+        for t in range(blocks)
+    ]
+    g_in[0].start()
+
+    for copy in p_send:
+        copy.wait_recv()
+    total = pars[0].astype(f32)
+    for o in range(1, 8):
+        total = total + pars[o].astype(f32)
+    par[...] = total
+    dk[...] = jnp.zeros_like(dk)
+    dv[...] = jnp.zeros_like(dv)
+    dw[...] = jnp.zeros_like(dw)
+    dwp[...] = jnp.zeros_like(dwp)
+    pgrad[...] = jnp.zeros_like(pgrad)
+    for i in range(3):
+        q_send[i].wait_recv()
+        q_pass[i].start()
+    q_send[3].wait_recv()
+    for copy in q_pass:
+        copy.wait_recv()
+
+    def first_act(rows):
+        unit, inverse = norm(tokens[rows].astype(f32))
+        return (unit * par[0:1] + par[1:2]).astype(bf16)
+
+    def project(b, _):
+        rows = rows_of(b)
+        r = mm(first_act(rows), flat_qkv[...]) + par[7:8]
+        qr[rows] = r[:, :WIDE].astype(bf16) * jnp.asarray(SCALE, bf16)
+        kr[rows] = r[:, WIDE : 2 * WIDE].astype(bf16)
+        v = r[:, 2 * WIDE :].astype(bf16)
+        vr[rows] = v
+        turned[:, rows] = v.T
+        return 0
+
+    lax.fori_loop(0, subs, project, 0)
+
+    def a_send(b, o):
+        return remote(
+            rows_all.at[m, b], rows_all.at[m, b], a_s.at[b, o], a_r.at[b, o], line[o]
+        )
+
+    def attend(t, _):
+        b = blocks - 1 - t
+        for half in (1, 0):
+            attend_block(2 * b + half, qr, kr, turned, starts, lse, orow, qs, acc)
+        top, low = rows_of(2 * b), rows_of(2 * b + 1)
+        rows_all[m, b, :QB] = orow[top, :128]
+        rows_all[m, b, QB : 2 * QB] = orow[low, :128]
+        rows_all[m, b, 2 * QB :] = (
+            orow[top, 128:].astype(f32) + pltpu.roll(orow[low, 128:].astype(f32), 64, 1)
+        ).astype(bf16)
+        for o in range(1, 4):
+            a_send(b, o).start()
+
+        @pl.when(t == 0)
+        def _():
+            advance(0, 1)
+            advance(1, 0)
+
+        @pl.when(t == 1)
+        def _():
+            advance(0, 2)
+            advance(1, 1)
+
+        @pl.when(t == 2)
+        def _():
+            advance(2, 0)
+            advance(1, 2)
+
+        return 0
+
+    lax.fori_loop(0, blocks, attend, 0)
+
+    def turn(i, _):
+        turned[:, rows_of(i)] = kr[rows_of(i)].T
+        return 0
+
+    lax.fori_loop(0, subs, turn, 0)
+    advance(2, 1)
+    advance(3, 0)
+    advance(2, 2)
+    advance(3, 1)
+    advance(3, 2)
+    for o in range(4):
+        for c in range(2):
+            hop(o, c, 2).wait_recv()
+
+    def bias_row(s, _):
+        wide = flat_fc[s, :, 896:1024].astype(f32)
+        fcb[s] = wide.T[64:65]
+        return 0
+
+    lax.fori_loop(0, 4, bias_row, 0)
+
+    end = (m == 0) | (m == 3)
+    inner = jnp.logical_not(end)
+    inward = (d, jnp.where(m < 2, 1, 2))
+    across = (d, 3 - m)
+    outward = (d, jnp.where(m < 2, 0, 3))
+
+    def hop_a(i):
+        return remote(part.at[i], edge.at[i], ar_s.at[0, i], ar_r.at[0, i], inward)
+
+    def hop_b(i):
+        return remote(part.at[i], far.at[i], ar_s.at[1, i], ar_r.at[1, i], across)
+
+    def hop_c(i):
+        return remote(edge.at[i], far.at[i], ar_s.at[2, i], ar_r.at[2, i], outward)
+
+    def stage_two(i):
+        @pl.when(inner)
+        def _():
+            hop_a(i).wait_recv()
+            part[i] = (part[i].astype(f32) + edge[i].astype(f32)).astype(bf16)
+            hop_b(i).start()
+
+    def stage_three(i):
+        @pl.when(inner)
+        def _():
+            hop_b(i).wait_recv()
+            edge[i] = (part[i].astype(f32) + far[i].astype(f32)).astype(bf16)
+            hop_c(i).start()
+
+    def gt_out(i):
+        return pltpu.make_async_copy(
+            hid.at[rows_of(i)], grad_tokens.at[rows_of(i)], g_s.at[8 + i]
+        )
+
+    def stage_four(i):
+        @pl.when(end)
+        def _():
+            hop_c(i).wait_recv()
+            edge[i] = far[i]
+
+        def finish(r, _):
+            some = rows_of(r, RB)
+            there = pl.ds(pl.multiple_of(i * QB + r * RB, RB), RB)
+            grad = edge[i, some].astype(f32)
+            unit, inverse = norm(tokens[there].astype(f32))
+            pgrad[0:1] += jnp.sum(grad * unit, axis=0, keepdims=True)
+            pgrad[1:2] += jnp.sum(grad, axis=0, keepdims=True)
+            back = norm_back(grad, par[0:1], unit, inverse)
+            hid[there] = (hid[there].astype(f32) + back).astype(bf16)
+            return 0
+
+        lax.fori_loop(0, QB // RB, finish, 0)
+        gt_out(i).start()
+
+    def out_copy(b, slot):
+        return pltpu.make_async_copy(gbuf.at[slot], output.at[rows_of(b, TB)], loc.at[2])
+
+    def block(t, _):
+        b = blocks - 1 - t
+        rows = rows_of(b, TB)
+        slot = lax.rem(t, 2)
+        pltpu.make_async_copy(grads.at[rows], gbuf.at[slot], loc.at[slot]).wait()
+
+        @pl.when(t >= 1)
+        def _():
+            out_copy(b + 1, 1 - slot).wait()
+
+        @pl.when(t < blocks - 1)
+        def _():
+            pltpu.make_async_copy(
+                grads.at[rows_of(b - 1, TB)], gbuf.at[1 - slot], loc.at[1 - slot]
+            ).start()
+
+        for o in range(1, 4):
+            a_send(b, o).wait_recv()
+
+        def head(s, _):
+            third = rows_all[s, b, 2 * QB :].astype(f32)
+            third = jnp.concatenate([third, pltpu.roll(third, 64, 1)], axis=0)
+            lane = lax.broadcasted_iota(jnp.int32, third.shape, 1)
+            third = jnp.where(lane < 64, third, 0.0).astype(bf16)
+            left = jnp.concatenate([rows_all[s, b, : 2 * QB], third], axis=1)
+            oacc[...] += mm(left, flat_fc[s, :, 768:1024], NT)
+            return 0
+
+        oacc[...] = tokens[rows].astype(f32) + par[4:5]
+        lax.fori_loop(0, 4, head, 0)
+
+        def second(r, _):
+            some = rows_of(r, RB)
+            hidden = oacc[some]
+            unit, inverse = norm(hidden)
+            normed[some] = unit
+            inv[some] = inverse
+            act[some] = (unit * par[2:3] + par[3:4]).astype(bf16)
+            oacc[some] = hidden + par[5:6]
+            gacc[some] = jnp.zeros_like(hidden)
+            return 0
+
+        lax.fori_loop(0, TB // RB, second, 0)
+
+        def slab(s, _):
+            def units(r, _):
+                some = rows_of(r)
+                pre = mm(act[some], flat_fc[s, :, 0:768]) + fcb[s]
+                back = mm(gbuf[slot, some], flat_out[s])
+                square = pre * pre
+                tangent = jnp.tanh(pre * (GELU_C + (GELU_C * 0.044715) * square))
+                half = 0.5 * pre
+                fired[some] = (half + half * tangent).astype(bf16)
+                slope = (0.5 + 0.5 * tangent) + half * (1.0 - tangent * tangent) * (
+                    GELU_C + (3.0 * GELU_C * 0.044715) * square
+                )
+                preg[some] = (back * slope).astype(bf16)
+                return 0
+
+            lax.fori_loop(0, TB // QB, units, 0)
+            oacc[...] += mm(fired[...], flat_out[s], NT)
+            gacc[...] += mm(preg[...], flat_fc[s, :, 0:768], NT)
+
+            @pl.when(s == m)
+            def _():
+                def outer(r, _):
+                    some = rows_of(r)
+                    dw[0, some] += mm(act[:, some], preg[...], TN)
+                    dw[1, some] += mm(gbuf[slot, :, some], fired[...], TN)
+                    return 0
+
+                lax.fori_loop(0, 3, outer, 0)
+                pgrad[6:7] += jnp.sum(preg[...].astype(f32), axis=0, keepdims=True)
+
+            @pl.when((s == 1) & (t >= 2))
+            def _():
+                stage_three(2 * b + 5)
+                stage_three(2 * b + 4)
+
+            return 0
+
+        lax.fori_loop(0, 4, slab, 0)
+
+        def rejoin(r, _):
+            some = rows_of(r, RB)
+            there = pl.ds(pl.multiple_of(b * TB + r * RB, RB), RB)
+            grad = gbuf[slot, some].astype(f32)
+            through, unit = gacc[some], normed[some]
+            pgrad[5:6] += jnp.sum(grad, axis=0, keepdims=True)
+            pgrad[2:3] += jnp.sum(through * unit, axis=0, keepdims=True)
+            pgrad[3:4] += jnp.sum(through, axis=0, keepdims=True)
+            branch = (grad + norm_back(through, par[2:3], unit, inv[some])).astype(bf16)
+            hid[there] = branch
+            pgrad[4:5] += jnp.sum(branch.astype(f32), axis=0, keepdims=True)
+            gbuf[slot, some] = oacc[some].astype(bf16)
+            return 0
+
+        lax.fori_loop(0, TB // RB, rejoin, 0)
+        out_copy(b, slot).start()
+        dwp[...] += mm(hid[rows], orow[rows], TN)
+        rowg[...] = mm(hid[rows], flat_fc[m, :, 768:1024]).astype(bf16)
+
+        @pl.when(t >= 1)
+        def _():
+            stage_two(2 * b + 3)
+            stage_two(2 * b + 2)
+
+        for half in (1, 0):
+            i = 2 * b + half
+            some = slice(half * QB, half * QB + QB)
+            attend_block_back(
+                i, rowg[some], qr, kr, vr, turned, orow, starts, lse, dk, dv, qs, gs, dqt
+            )
+            stacked[some, :WIDE] = (dqt[...].T * SCALE).astype(bf16)
+            stacked[some, WIDE : 2 * WIDE] = dk[rows_of(i)].astype(bf16)
+            stacked[some, 2 * WIDE :] = dv[rows_of(i)].astype(bf16)
+            part[i] = mm(stacked[some], flat_qkv[...], NT).astype(bf16)
+
+            @pl.when(end)
+            def _():
+                hop_a(i).start()
+
+        pgrad[7:8] += jnp.sum(stacked[...].astype(f32), axis=0, keepdims=True)
+        def again(r, _):
+            act[rows_of(r, RB)] = first_act(pl.ds(pl.multiple_of(b * TB + r * RB, RB), RB))
+            return 0
+
+        lax.fori_loop(0, TB // RB, again, 0)
+
+        def outer(r, _):
+            some = rows_of(r)
+            dw[2, some] += mm(act[:, some], stacked[...], TN)
+            return 0
+
+        lax.fori_loop(0, 3, outer, 0)
+
+        @pl.when(t >= 2)
+        def _():
+            stage_four(2 * b + 5)
+            stage_four(2 * b + 4)
+
+        return 0
+
+    lax.fori_loop(0, blocks, block, 0)
+
+    for c in range(2):
+        for o in range(3):
+            z_send[c][o].wait_send()
+        for o in range(4):
+            for stage in range(3):
+                hop(o, c, stage).wait_send()
+    for device in (x_dev, y_dev, diag, twin):
+        pl.semaphore_signal(free, inc=1, device_id=device, device_id_type=MESH)
+    sib = w_fc.at[:, :, :, 0, :, 0:768]
+
+    def rbuf(i):
+        return w_fc.at[:, i // 2, i % 2, 1, :, 0:768]
+
+    def pieces(yy, xx, kk):
+        return w_out.at[:, yy, xx, kk]
+
+    def take(c, dest):
+        if c < 3:
+            return dw[c, pl.ds(pl.multiple_of(dest * 96, 96), 96)]
+        return dwp[pl.ds(pl.multiple_of(dest * 96, 96), 96)]
+
+    spans = (768, 768, 768, 256)
+    for yy in range(2):
+        for xx in range(2):
+            for c in range(4):
+                w_out[c, yy, xx, 1 - k, :, : spans[c]] = take(c, yy * 4 + xx * 2 + 1 - k).astype(bf16)
+    twin_copy = remote(w_out.at[:, :, :, 1 - k], sib, d_s.at[0], d_r.at[0], twin)
+    pl.semaphore_wait(free, 4)
+    twin_copy.start()
+    stage_two(1)
+    stage_three(3)
+    stage_three(2)
+    twin_copy.wait_recv()
+    wants = [(y, 1 - x, x_dev), (1 - y, x, y_dev), (1 - y, 1 - x, diag)]
+    owner_copies = []
+    for i, (yy, xx, device) in enumerate(wants):
+        for c in range(4):
+            w_out[c, yy, xx, k, :, : spans[c]] = (
+                take(c, yy * 4 + xx * 2 + k) + w_fc[c, yy, xx, 0, :, : spans[c]].astype(f32)
+            ).astype(bf16)
+        copy = remote(pieces(yy, xx, k), rbuf(i), d_s.at[1 + i], d_r.at[1 + i], device)
+        copy.start()
+        owner_copies.append(copy)
+    stage_two(0)
+    stage_three(1)
+    stage_four(3)
+    stage_four(2)
+    stage_three(0)
+    for copy in owner_copies:
+        copy.wait_recv()
+    for c in range(4):
+        value = take(c, d) + w_fc[c, y, x, 0, :, : spans[c]].astype(f32)
+        for i in range(3):
+            value = value + w_fc[c, i // 2, i % 2, 1, :, : spans[c]].astype(f32)
+        if c < 3:
+            dw[c, pl.ds(pl.multiple_of(d * 96, 96), 96)] = value
+        else:
+            dwp[pl.ds(pl.multiple_of(d * 96, 96), 96)] = value
+    results = [
+        pltpu.make_async_copy(
+            dw.at[:, pl.ds(pl.multiple_of(d * 96, 96), 96)], dw_out, loc.at[3]
+        ),
+        pltpu.make_async_copy(dwp.at[pl.ds(pl.multiple_of(d * 96, 96), 96)], dwp_out, loc.at[4]),
+    ]
+    for copy in results:
+        copy.start()
+    stage_four(1)
+    stage_four(0)
+
+    g_send = [
+        remote(pgrad, pgbuf.at[o], g_s.at[o], g_r.at[o], plane[o]) for o in range(1, 8)
+    ]
+    for copy in g_send:
+        copy.start()
+    total = pgrad[...]
+    for o, copy in enumerate(g_send):
+        copy.wait_recv()
+    for o in range(1, 8):
+        total = total + pgbuf[o]
+    pg_out[...] = total
+
+    for copy in results:
+        copy.wait()
+    for copy in g_send + q_send + q_pass + p_send + owner_copies + [twin_copy]:
+        copy.wait_send()
+    out_copy(0, (blocks - 1) % 2).wait()
+
+    def leave(i, _):
+        gt_out(i).wait()
+
+        @pl.when(end)
+        def _():
+            hop_a(i).wait_send()
+
+        @pl.when(inner)
+        def _():
+            hop_b(i).wait_send()
+            hop_c(i).wait_send()
+
+        return 0
+
+    lax.fori_loop(0, subs, leave, 0)
+    for b in range(blocks):
+        for o in range(1, 4):
+            a_send(b, o).wait_send()
+
+
+def whole_block(tokens, out_grad, starts, fc_own, out_own, qkv_own, par_own):
+    count = tokens.shape[0]
+    blocks, subs = count // TB, count // QB
+    any_space = pl.BlockSpec(memory_space=pl.ANY)
+    dma = pltpu.SemaphoreType.DMA
+    return pl.pallas_call(
+        whole_kernel,
+        out_shape=(
+            jax.ShapeDtypeStruct((count, 768), bf16),
+            jax.ShapeDtypeStruct((count, 768), bf16),
+            jax.ShapeDtypeStruct((3, 96, 768), f32),
+            jax.ShapeDtypeStruct((96, WIDE), f32),
+            jax.ShapeDtypeStruct((8, 768), f32),
+        ),
+        in_specs=[VMEM, any_space] + [VMEM] * 5,
+        out_specs=(any_space, any_space, any_space, any_space, VMEM),
+        scratch_shapes=[
+            pltpu.VMEM((4, 2, 2, 2, 96, 1024), bf16),
+            pltpu.VMEM((4, 2, 2, 2, 96, 768), bf16),
+            pltpu.VMEM((2, 2, 2, 96, 768), bf16),
+            pltpu.VMEM((8, 16, 768), bf16),
+            pltpu.VMEM((16, 768), f32),
+            pltpu.VMEM((4, 1, 768), f32),
+            pltpu.VMEM((count, WIDE), bf16),
+            pltpu.VMEM((count, WIDE), bf16),
+            pltpu.VMEM((count, WIDE), bf16),
+            pltpu.VMEM((WIDE, count), bf16),
+            pltpu.VMEM((count, WIDE), bf16),
+            pltpu.VMEM((4, blocks, 3 * QB, 128), bf16),
+            pltpu.VMEM((subs, 1, HPD * QB), f32),
+            pltpu.VMEM((HPD * QB, WIDE), bf16),
+            pltpu.VMEM((HPD * QB, WIDE), bf16),
+            pltpu.VMEM((HD, HPD * QB), f32),
+            pltpu.VMEM((WIDE, QB), f32),
+            pltpu.VMEM((count, WIDE), f32),
+            pltpu.VMEM((count, WIDE), f32),
+            pltpu.VMEM((2, TB, 768), bf16),
+            pltpu.VMEM((TB, 768), f32),
+            pltpu.VMEM((TB, 1), f32),
+            pltpu.VMEM((TB, 768), bf16),
+            pltpu.VMEM((TB, 768), f32),
+            pltpu.VMEM((TB, 768), f32),
+            pltpu.VMEM((TB, 768), bf16),
+            pltpu.VMEM((TB, 768), bf16),
+            pltpu.VMEM((TB, WIDE), bf16),
+            pltpu.VMEM((TB, 768), bf16),
+            pltpu.VMEM((count, 768), bf16),
+            pltpu.VMEM((3, 768, 768), f32),
+            pltpu.VMEM((768, 256), f32),
+            pltpu.VMEM((8, 768), f32),
+            pltpu.VMEM((8, 8, 768), f32),
+            pltpu.VMEM((subs, QB, 768), bf16),
+            pltpu.VMEM((subs, QB, 768), bf16),
+            pltpu.VMEM((subs, QB, 768), bf16),
+            dma((7,)),
+            dma((7,)),
+            dma((8,)),
+            dma((8,)),
+            dma((2, 4)),
+            dma((2, 4)),
+            dma((2, 3, 4)),
+            dma((2, 3, 4)),
+            dma((blocks, 4)),
+            dma((blocks, 4)),
+            dma((3, subs)),
+            dma((3, subs)),
+            dma((4,)),
+            dma((4,)),
+            dma((8 + subs,)),
+            dma((8,)),
+            dma((5,)),
+            pltpu.SemaphoreType.REGULAR,
+        ],
+        compiler_params=pltpu.CompilerParams(
+            collective_id=0, has_side_effects=True, vmem_limit_bytes=63 * 2**20
+        ),
+    )(tokens, out_grad, starts, fc_own, out_own, qkv_own, par_own)
+
+
+def per_device_whole(
+    tokens,
+    lengths,
+    first_gain,
+    first_shift,
+    qkv_weight,
+    qv_bias,
+    proj_weight,
+    proj_bias,
+    second_gain,
+    second_shift,
+    fc_weight,
+    fc_bias,
+    out_weight,
+    out_bias,
+    out_grad,
+):
+    d = lax.axis_index("dp")
+    starts = segment_starts(lengths[0], tokens.shape[0])
+    fc_own = jnp.concatenate(
+        [fc_weight, proj_weight.T, fc_bias.T, jnp.zeros((96, 63), bf16)], axis=1
+    )
+    out_own = out_weight.T
+    qkv_own = jnp.pad(qkv_weight, ((0, 0), (0, 0), (0, WIDE - 192)))
+    qkv_own = jnp.moveaxis(qkv_own, 0, 1).reshape(96, 3 * WIDE)
+    vectors = jnp.stack(
+        [first_gain, first_shift, second_gain, second_shift, proj_bias, out_bias, fc_bias[0]]
+    )
+    par_own = jnp.zeros((16, 768), bf16)
+    par_own = lax.dynamic_update_slice(par_own, vectors, (0, 96 * d))
+    par_own = lax.dynamic_update_slice(par_own, qv_bias[0], (7, 24 * d))
+    par_own = lax.dynamic_update_slice(par_own, qv_bias[1], (7, 2 * WIDE + 24 * d))
+    output, grad_tokens, dw, dwp, pg = whole_block(
+        tokens, out_grad, starts, fc_own, out_own, qkv_own, par_own
+    )
+    vec = lax.dynamic_slice(pg, (0, 96 * d), (7, 96))
+    qv = jnp.concatenate(
+        [
+            lax.dynamic_slice(pg, (7, 24 * d), (1, 24)),
+            lax.dynamic_slice(pg, (7, 2 * WIDE + 24 * d), (1, 24)),
+        ]
+    )[:, None, :]
+    qkv_grad = jnp.moveaxis(dw[2].reshape(96, 3, WIDE)[:, :, :192], 1, 0)
+    return (
+        output,
+        grad_tokens,
+        vec[0],
+        vec[1],
+        qkv_grad,
+        qv,
+        dwp[:, :192].T,
+        vec[4],
+        vec[2],
+        vec[3],
+        dw[0],
+        vec[6][None],
+        dw[1].T,
+        vec[5],
+    )
+
+
 def solution(mesh):
     placed = (
         P("dp", None),
@@ -415,7 +1131,7 @@
         P("dp", None),
     )
     return jax.shard_map(
-        per_device,
+        per_device_whole if dict(mesh.shape) == {"dp": 8, "mp": 4} else per_device,
         mesh=mesh,
         in_specs=placed,
         out_specs=(

time: 721 us -> 270 us (0.37); the launches traced: 711 us -> 269 us
  waiting for transfers between devices: 362 us -> 0 us
  Pallas kernels: 44.5 us -> 247 us
  blocking collectives: 88.1 us -> 0 us
  matrix products: 65.9 us -> 0 us
  other arithmetic: 56.1 us -> 3.11 us
  local copies, waits for them, and re-layouts: 51.6 us -> 18.8 us
  starting transfers between devices: 25.5 us -> 0 us
  between operations: 17.7 us -> 0.74 us
    psum x3 -> x0, waiting for transfers between devices: 357 us -> none  [the longest x1 125 us: per_device(): lax.psum(jnp.dot(fired, out_all, preferred_element_type=jnp.float32).asty...]
    pallas_call x2 -> x1, Pallas kernels: 44.5 us -> 247 us  [whole_block(): pl.pallas_call(whole_kernel, out_shape=(jax.ShapeDtypeStruct((count, 768)...]
    dot_general x11 -> x0, matrix products: 60.6 us -> none  [the longest x1 9.73 us: per_device(): jnp.dot(act_two, fc_all, preferred_element_type=jnp.float32)]
    unnamed x2 -> x0, blocking collectives: 55.2 us -> none
    reduce_sum x16 -> x0, other arithmetic: 37.7 us -> none  [the longest x1 6.98 us: per_device(): gain_two_grad = jnp.sum(act_two_grad * normed_two, axis=0)]
    all_gather x3 -> x0, blocking collectives: 32.9 us -> none  [the longest x1 14.1 us: per_device(): lax.all_gather(qkv_weight, 'dp', axis=1, tiled=True)]
    all_to_all x6 -> x0, starting transfers between devices: 24.3 us -> none  [summed_on_arrival(): pieces = lax.all_to_all(split_up(shard, dim, size), axis, 0, 0, tiled=True)]
    unnamed x86 -> x12, local copies, waits for them, and re-layouts: 26.7 us -> 8.03 us
  transfers between devices with their start and end apart: 14 -> 0, of which waited for: 4 -> 0; matrix products, arithmetic and copies ran while one was open for 15% -> 0% of each run, Pallas kernels for 3% -> 0%
where the time goes in v2:
time: 270 us; the launch traced here: 269 us
  Pallas kernels  247 us (91%)
  local copies, waits for them, and re-layouts  18.8 us (7%)
  other arithmetic  3.11 us (1%)
    pallas_call x1, Pallas kernels, whole_block(): pl.pallas_call(whole_kernel, out_shape=(jax.ShapeDtypeStruct((count, 768)...  247 us
    unnamed x12, local copies, waits for them, and re-layouts  8.03 us

profile of v2, /device:TPU:0, one launch (start us, length us, event | category | flops | bytes accessed | tf_op | source)
XLA Modules:
  0.0 269.3 jit_solution(12934783902304740256)
XLA Ops:
  0.7 0.8 stack.27
  1.4 0.3 dynamic_update_slice.9
  1.8 0.7 slice_bitcast_fusion.10
  2.6 0.2 dynamic_update_slice.11.par_own
  2.8 0.9 pad_bitcast_fusion
  3.7 0.7 copy.50
  4.4 0.9 copy.44
  5.3 0.8 copy.45
  6.2 1.7 maximum_maximum_fusion.fc_own
  7.8 0.7 copy.43
  8.7 0.7 select_reduce_fusion
  9.4 246.7 %shard_map.254 = (bf16[2048,768]{1,0:T(8,128)(2,1)}, bf16[2048,768]{1,0:T(8,128)(2,1)}, f32[3,96,768]{2,1,0:T(8,128)}, f32[96,256]{1,0:T(8,128)}, f32[8,768]{1,0:T(8,128)}) custom-call(bf16[2048,768]{1,0:T(8,128)(2,1)} %tokens.1, bf16[2048,768]{1,0:T(8,128)(2,1)} %grads.1, s32[1,2048]{1,0:T(1,128)} %bitcast.47, bf16[96,1024]{1,0:T(8,128)(2,1)} %maximum_maximum_fusion.fc_own, ...), custom_call_target="tpu_custom_call" | custom-call | tf_op jit(solution)/shard_map/pallas_call | solution.py:980
  256.1 0.9 constant_dynamic-slice_fusion.1
  257.1 0.6 pad_maximum_fusion
  257.6 0.8 constant_dynamic-slice_fusion.2
  258.4 0.5 slice_bitcast_fusion.4
  258.9 2.1 slice_bitcast_fusion.1
  261.0 1.1 reshape_squeeze.3
  262.2 0.8 copy.47
  263.0 0.9 slice_bitcast_fusion.3
  263.9 0.7 copy.49
  264.6 1.7 copy.56
  266.3 1.4 copy-done
  267.6 1.7 copy.57
  (12 shorter events, 0.4 us)
Async XLA Ops:
  2.8 6.6 %copy-start.2 = (bf16[16,768]{1,0:T(8,128)(2,1)}, bf16[16,768]{1,0:T(8,128)(2,1)S(1)}, u32[]{:S(2)}) copy-start(bf16[16,768]{1,0:T(8,128)(2,1)S(1)} %dynamic_update_slice.11.par_own) | copy-start | bytes 73732
  256.1 8.5 %copy-start.1 = (bf16[2048,768]{1,0:T(8,128)(2,1)S(1)}, bf16[2048,768]{1,0:T(8,128)(2,1)}, u32[]{:S(2)}) copy-start(bf16[2048,768]{1,0:T(8,128)(2,1)} %get-tuple-element.94) | copy-start | bytes 9437188
  264.6 3.0 %copy-start = (bf16[2048,768]{1,0:T(8,128)(2,1)S(1)}, bf16[2048,768]{1,0:T(8,128)(2,1)}, u32[]{:S(2)}) copy-start(bf16[2048,768]{1,0:T(8,128)(2,1)} %get-tuple-element.95) | copy-start | bytes 9437188

commit v3 on v2

--- a/solution.py
+++ b/solution.py
@@ -420,6 +420,7 @@
     starts,
     fc_own,
     out_own,
+    pr_own,
     qkv_own,
     par_own,
     output,
@@ -429,6 +430,7 @@
     pg_out,
     w_fc,
     w_out,
+    w_pr,
     w_qkv,
     pars,
     par,
@@ -461,6 +463,7 @@
     dwp,
     pgrad,
     pgbuf,
+    zgbuf,
     part,
     edge,
     far,
@@ -472,12 +475,15 @@
     z_r,
     w_s,
     w_r,
+    af_s,
     a_s,
     a_r,
     ar_s,
     ar_r,
     d_s,
     d_r,
+    zg_s,
+    zg_r,
     g_s,
     g_r,
     loc,
@@ -492,7 +498,8 @@
     def place(yy, xx, kk):
         return (yy * 4 + xx * 2 + kk, m)
 
-    flat_fc = w_fc.reshape(4, 768, 1024)
+    flat_fc = w_fc.reshape(4, 768, 768)
+    flat_pr = w_pr.reshape(4, 768, 256)
     flat_out = w_out.reshape(4, 768, 768)
     flat_qkv = w_qkv.reshape(768, 3 * WIDE)
     x_dev, y_dev, diag, twin = (
@@ -503,7 +510,10 @@
     )
     plane = [(lax.rem(d + o, 8), m) for o in range(8)]
     line = [(d, lax.rem(m + o, 4)) for o in range(4)]
-    came = [lax.rem(m + 4 - o, 4) for o in range(4)]
+    above, below = (d, jnp.minimum(m + 1, 3)), (d, jnp.maximum(m - 1, 0))
+    end = (m == 0) | (m == 3)
+    inner = jnp.logical_not(end)
+    order = [m] + [jnp.where(m <= o - 1, o, o - 1) for o in range(1, 4)]
 
     barrier = pltpu.get_barrier_semaphore()
     for device in plane[1:] + line[1:]:
@@ -524,52 +534,68 @@
     p_send = [remote(par_own, pars.at[o], p_s.at[o], p_r.at[o], plane[o]) for o in range(1, 8)]
     for copy in p_send:
         copy.start()
-    own = (fc_own, out_own)
-    held = (w_fc, w_out)
-    z_send = [
-        [
-            remote(own[c], held[c].at[m, y, x, k], z_s.at[c, o], z_r.at[c, o], line[o])
-            for o in range(1, 4)
-        ]
-        for c in range(2)
-    ]
-    for o in range(3):
-        for c in range(2):
-            z_send[c][o].start()
     w_fc[m, y, x, k] = fc_own[...]
     w_out[m, y, x, k] = out_own[...]
+    w_pr[m, y, x, k] = pr_own[...]
     w_qkv[y, x, k] = qkv_own[...]
     pars[0] = par_own[...]
-
-    def hop(o, c, stage):
-        s = came[o]
+    held = (w_fc, w_out, w_pr)
+
+    def along(piece, send, recv, s):
+        up = remote(piece, piece, send.at[0], recv, above)
+        down = remote(piece, piece, send.at[1], recv, below)
+        return ((s <= m) & (m < 3), up), ((s >= m) & (m > 0), down)
+
+    def pass_on(piece, send, recv, s):
+        for where, copy in along(piece, send, recv, s):
+            pl.when(where)(copy.start)
+
+    def passed_on(piece, send, recv, s):
+        for where, copy in along(piece, send, recv, s):
+            pl.when(where)(copy.wait_send)
+
+    def z_args(c, s):
+        return held[c].at[s, y, x, k], z_s.at[c, s], z_r.at[c, s], s
+
+    def z_step(cs, far_by):
+        for s, there in ((m - far_by, m >= far_by), (m + far_by, m + far_by <= 3)):
+
+            @pl.when(there)
+            def _():
+                for c in cs:
+                    piece, send, recv, _ = z_args(c, s)
+                    remote(piece, piece, send.at[0], recv, above).wait_recv()
+                    pass_on(*z_args(c, s))
+                if 0 in cs:
+                    spread(s, cs)
+
+    for c in (2, 0, 1):
+        pass_on(*z_args(c, m))
+
+    def hop(s, c, stage):
         if stage == 0:
             part_of = held[c].at[s, y, x, k]
-            device = (x_dev, y_dev)[c]
+            device = y_dev if c == 1 else x_dev
         elif stage == 1:
-            part_of = (held[0].at[s, y, :, k], held[1].at[s, :, x, k])[c]
-            device = (y_dev, x_dev)[c]
+            part_of = held[c].at[s, :, x, k] if c == 1 else held[c].at[s, y, :, k]
+            device = x_dev if c == 1 else y_dev
         else:
             part_of = held[c].at[s, :, :, k]
             device = twin
-        return remote(part_of, part_of, w_s.at[c, stage, o], w_r.at[c, stage, o], device)
-
-    def advance(o, stage):
-        for c in range(2):
-            if stage > 0:
-                hop(o, c, stage - 1).wait_recv()
-            elif o > 0:
-                z_send[c][o - 1].wait_recv()
-            hop(o, c, stage).start()
-
-    advance(0, 0)
-    g_in = [
-        pltpu.make_async_copy(
-            grads.at[pl.ds((blocks - 1 - t) * TB, TB)], gbuf.at[t % 2], loc.at[t % 2]
-        )
-        for t in range(blocks)
-    ]
-    g_in[0].start()
+        return remote(part_of, part_of, w_s.at[c, stage, s], w_r.at[c, stage, s], device)
+
+    def spread(s, cs=(0, 1)):
+        for c in cs:
+            hop(s, c, 0).start()
+
+    def advance(o, stage, cs=(0, 1)):
+        for c in cs:
+            hop(order[o], c, stage - 1).wait_recv()
+            hop(order[o], c, stage).start()
+
+    pltpu.make_async_copy(
+        grads.at[rows_of(blocks - 1, TB)], gbuf.at[0], loc.at[0]
+    ).start()
 
     for copy in p_send:
         copy.wait_recv()
@@ -582,9 +608,16 @@
     dw[...] = jnp.zeros_like(dw)
     dwp[...] = jnp.zeros_like(dwp)
     pgrad[...] = jnp.zeros_like(pgrad)
+    z_step((2,), 1)
+    z_step((2,), 2)
+    z_step((2,), 3)
     for i in range(3):
         q_send[i].wait_recv()
         q_pass[i].start()
+    spread(m)
+    for s in range(4):
+        spread(s, (2,))
+    z_step((0, 1), 1)
     q_send[3].wait_recv()
     for copy in q_pass:
         copy.wait_recv()
@@ -601,70 +634,104 @@
         v = r[:, 2 * WIDE :].astype(bf16)
         vr[rows] = v
         turned[:, rows] = v.T
+
+        @pl.when(b == 0)
+        def _():
+            advance(0, 1)
+
+        @pl.when(b == 2)
+        def _():
+            for o in range(4):
+                advance(o, 1, (2,))
+
+        @pl.when(b == 4)
+        def _():
+            z_step((0, 1), 2)
+
+        @pl.when(b == 6)
+        def _():
+            for o in range(4):
+                advance(o, 2, (2,))
+
         return 0
 
     lax.fori_loop(0, subs, project, 0)
 
-    def a_send(b, o):
-        return remote(
-            rows_all.at[m, b], rows_all.at[m, b], a_s.at[b, o], a_r.at[b, o], line[o]
-        )
+    def a_args(b, s):
+        return rows_all.at[s, b], a_s.at[b, s], a_r.at[b, s], s
+
+    def a_wait(b, s):
+        piece, send, recv, _ = a_args(b, s)
+        remote(piece, piece, send.at[0], recv, above).wait_recv()
+
+    def a_step(b, far_by):
+        for s, there in ((m - far_by, m >= far_by), (m + far_by, m + far_by <= 3)):
+
+            @pl.when(there & inner)
+            def _():
+                a_wait(b, s)
+                pass_on(*a_args(b, s))
+
+    def direct(b, o):
+        return remote(rows_all.at[m, b], rows_all.at[m, b], af_s.at[o], a_r.at[b, m], line[o])
 
     def attend(t, _):
         b = blocks - 1 - t
-        for half in (1, 0):
-            attend_block(2 * b + half, qr, kr, turned, starts, lse, orow, qs, acc)
+        attend_block(2 * b + 1, qr, kr, turned, starts, lse, orow, qs, acc)
+
+        @pl.when(t == 0)
+        def _():
+            advance(0, 2)
+
+        @pl.when(t == 1)
+        def _():
+            advance(1, 1)
+
+        @pl.when(t == 2)
+        def _():
+            advance(3, 1)
+
+        attend_block(2 * b, qr, kr, turned, starts, lse, orow, qs, acc)
         top, low = rows_of(2 * b), rows_of(2 * b + 1)
         rows_all[m, b, :QB] = orow[top, :128]
         rows_all[m, b, QB : 2 * QB] = orow[low, :128]
         rows_all[m, b, 2 * QB :] = (
             orow[top, 128:].astype(f32) + pltpu.roll(orow[low, 128:].astype(f32), 64, 1)
         ).astype(bf16)
-        for o in range(1, 4):
-            a_send(b, o).start()
 
         @pl.when(t == 0)
         def _():
-            advance(0, 1)
-            advance(1, 0)
+            z_step((0, 1), 3)
+            for o in range(1, 4):
+                direct(blocks - 1, o).start()
+
+        @pl.when(t > 0)
+        def _():
+            pass_on(*a_args(b, m))
 
         @pl.when(t == 1)
         def _():
-            advance(0, 2)
-            advance(1, 1)
-
-        @pl.when(t == 2)
-        def _():
-            advance(2, 0)
-            advance(1, 2)
+            advance(2, 1)
 
         return 0
 
     lax.fori_loop(0, blocks, attend, 0)
+    advance(1, 2)
 
     def turn(i, _):
         turned[:, rows_of(i)] = kr[rows_of(i)].T
         return 0
 
     lax.fori_loop(0, subs, turn, 0)
-    advance(2, 1)
-    advance(3, 0)
-    advance(2, 2)
-    advance(3, 1)
-    advance(3, 2)
-    for o in range(4):
-        for c in range(2):
-            hop(o, c, 2).wait_recv()
+    for s in range(4):
+        hop(s, 2, 2).wait_recv()
 
     def bias_row(s, _):
-        wide = flat_fc[s, :, 896:1024].astype(f32)
-        fcb[s] = wide.T[64:65]
+        fcb[s] = flat_pr[s, :, 128:256].astype(f32).T[64:65]
         return 0
 
     lax.fori_loop(0, 4, bias_row, 0)
 
-    end = (m == 0) | (m == 3)
-    inner = jnp.logical_not(end)
     inward = (d, jnp.where(m < 2, 1, 2))
     across = (d, 3 - m)
     outward = (d, jnp.where(m < 2, 0, 3))
@@ -694,7 +761,7 @@
 
     def gt_out(i):
         return pltpu.make_async_copy(
-            hid.at[rows_of(i)], grad_tokens.at[rows_of(i)], g_s.at[8 + i]
+            hid.at[rows_of(i, RB)], grad_tokens.at[rows_of(i, RB)], g_s.at[8 + i]
         )
 
     def stage_four(i):
@@ -703,254 +770,409 @@
             hop_c(i).wait_recv()
             edge[i] = far[i]
 
-        def finish(r, _):
-            some = rows_of(r, RB)
-            there = pl.ds(pl.multiple_of(i * QB + r * RB, RB), RB)
-            grad = edge[i, some].astype(f32)
-            unit, inverse = norm(tokens[there].astype(f32))
-            pgrad[0:1] += jnp.sum(grad * unit, axis=0, keepdims=True)
-            pgrad[1:2] += jnp.sum(grad, axis=0, keepdims=True)
-            back = norm_back(grad, par[0:1], unit, inverse)
-            hid[there] = (hid[there].astype(f32) + back).astype(bf16)
-            return 0
-
-        lax.fori_loop(0, QB // RB, finish, 0)
+        there = rows_of(i, RB)
+        grad = edge[i].astype(f32)
+        unit, inverse = norm(tokens[there].astype(f32))
+        back = norm_back(grad, par[0:1], unit, inverse)
+        hid[there] = (hid[there].astype(f32) + back).astype(bf16)
         gt_out(i).start()
 
     def out_copy(b, slot):
         return pltpu.make_async_copy(gbuf.at[slot], output.at[rows_of(b, TB)], loc.at[2])
 
-    def block(t, _):
-        b = blocks - 1 - t
-        rows = rows_of(b, TB)
-        slot = lax.rem(t, 2)
-        pltpu.make_async_copy(grads.at[rows], gbuf.at[slot], loc.at[slot]).wait()
-
-        @pl.when(t >= 1)
-        def _():
-            out_copy(b + 1, 1 - slot).wait()
-
-        @pl.when(t < blocks - 1)
-        def _():
-            pltpu.make_async_copy(
-                grads.at[rows_of(b - 1, TB)], gbuf.at[1 - slot], loc.at[1 - slot]
-            ).start()
-
-        for o in range(1, 4):
-            a_send(b, o).wait_recv()
-
-        def head(s, _):
-            third = rows_all[s, b, 2 * QB :].astype(f32)
-            third = jnp.concatenate([third, pltpu.roll(third, 64, 1)], axis=0)
-            lane = lax.broadcasted_iota(jnp.int32, third.shape, 1)
-            third = jnp.where(lane < 64, third, 0.0).astype(bf16)
-            left = jnp.concatenate([rows_all[s, b, : 2 * QB], third], axis=1)
-            oacc[...] += mm(left, flat_fc[s, :, 768:1024], NT)
+    def out_half(i):
+        return pltpu.make_async_copy(
+            gbuf.at[(blocks - 1) % 2, rows_of(i)], output.at[rows_of(i)], loc.at[5 + i]
+        )
+
+    groups = ((0, 1), (2,), (3,))
+    spans = (768, 768, 768, 256)
+    wants = [(y, 1 - x, x_dev), (1 - y, x, y_dev), (1 - y, 1 - x, diag)]
+
+    def take(c, dest):
+        some = pl.ds(pl.multiple_of(dest * 96, 96), 96)
+        return dw[c, some] if c < 3 else dwp[some]
+
+    def span_of(ref, g, *rest):
+        if g == 0:
+            return ref.at[(slice(0, 2),) + rest]
+        return ref.at[(g + 1,) + rest + ((slice(None), slice(0, 256)) if g == 2 else ())]
+
+    def twin_sum(g):
+        every = (slice(None), slice(None))
+        return remote(
+            span_of(w_out, g, *every, 1 - k), span_of(w_fc, g, *every, 0), d_s.at[g], d_r.at[g], twin
+        )
+
+    def to_owner(g, i):
+        yy, xx, device = wants[i]
+        n = 3 + 3 * i + g
+        return remote(
+            span_of(w_out, g, yy, xx, k),
+            span_of(w_fc, g, i // 2, i % 2, 1),
+            d_s.at[n],
+            d_r.at[n],
+            device,
+        )
+
+    def give_twin(g):
+        for yy in range(2):
+            for xx in range(2):
+                for c in groups[g]:
+                    w_out[c, yy, xx, 1 - k, :, : spans[c]] = take(
+                        c, yy * 4 + xx * 2 + 1 - k
+                    ).astype(bf16)
+
+    def give_owners(g):
+        twin_sum(g).wait_recv()
+        for i, (yy, xx, _) in enumerate(wants):
+            for c in groups[g]:
+                w_out[c, yy, xx, k, :, : spans[c]] = (
+                    take(c, yy * 4 + xx * 2 + k) + w_fc[c, yy, xx, 0, :, : spans[c]].astype(f32)
+                ).astype(bf16)
+            to_owner(g, i).start()
+
+    def result(c):
+        some = pl.ds(pl.multiple_of(d * 96, 96), 96)
+        return (
+            pltpu.make_async_copy(dw.at[c, some], dw_out.at[c], loc.at[7 + c])
+            if c < 3
+            else pltpu.make_async_copy(dwp.at[some], dwp_out, loc.at[10])
+        )
+
+    def own_sum(g):
+        for i in range(3):
+            to_owner(g, i).wait_recv()
+        some = pl.ds(pl.multiple_of(d * 96, 96), 96)
+        for c in groups[g]:
+            value = take(c, d) + w_fc[c, y, x, 0, :, : spans[c]].astype(f32)
+            for i in range(3):
+                value = value + w_fc[c, i // 2, i % 2, 1, :, : spans[c]].astype(f32)
+            if c < 3:
+                dw[c, some] = value
+            else:
+                dwp[some] = value
+            result(c).start()
+
+    def make_block(size):
+        big = size == TB
+        all_rows = slice(0, size)
+
+        def block(t, _):
+            b = blocks - 1 - t if big else 0
+            i_last = 2 * b + 1 if big else 1 - t
+            row = b * TB if big else (1 - t) * QB
+            off = 0 if big else (1 - t) * QB
+            rows = pl.ds(pl.multiple_of(row, QB), size)
+            slot = lax.rem(t, 2) if big else (blocks - 1) % 2
+            g_rows = pl.ds(pl.multiple_of(off, QB), size)
+
+            def part_of(r, step):
+                return pl.ds(pl.multiple_of(off + r * step, step), step)
+
+            @pl.when((t >= 0) if big else (t == 0))
+            def _():
+                pltpu.make_async_copy(
+                    grads.at[rows_of(b, TB)], gbuf.at[slot], loc.at[slot]
+                ).wait()
+
+            if big:
+
+                @pl.when(t >= 1)
+                def _():
+                    out_copy(b + 1, 1 - slot).wait()
+
+                pltpu.make_async_copy(
+                    grads.at[rows_of(b - 1, TB)], gbuf.at[1 - slot], loc.at[1 - slot]
+                ).start()
+
+            for s in range(4):
+
+                @pl.when((end | (b == blocks - 1)) & (m != s) & ((t >= 0) if big else (t == 0)))
+                def _():
+                    a_wait(b, s)
+
+            def head(s, _):
+                third = rows_all[s, b, 2 * QB :].astype(f32)
+                turned_third = pltpu.roll(third, 64, 1)
+                if big:
+                    third = jnp.concatenate([third, turned_third], axis=0)
+                else:
+                    third = jnp.where(t == 0, turned_third, third)
+                lane = lax.broadcasted_iota(jnp.int32, third.shape, 1)
+                third = jnp.where(lane < 64, third, 0.0).astype(bf16)
+                left = jnp.concatenate([rows_all[s, b, g_rows], third], axis=1)
+                oacc[all_rows] += mm(left, flat_pr[s], NT)
+                return 0
+
+            oacc[all_rows] = tokens[rows].astype(f32) + par[4:5]
+            lax.fori_loop(0, 4, head, 0)
+
+            def second(r, _):
+                some = rows_of(r, RB)
+                hidden = oacc[some]
+                unit, inverse = norm(hidden)
+                normed[some] = unit
+                inv[some] = inverse
+                act[some] = (unit * par[2:3] + par[3:4]).astype(bf16)
+                oacc[some] = hidden + par[5:6]
+                gacc[some] = jnp.zeros_like(hidden)
+                return 0
+
+            lax.fori_loop(0, size // RB, second, 0)
+
+            def slab(s, _):
+                if big:
+
+                    @pl.when(t == 0)
+                    def _():
+                        for c in range(2):
+                            hop(s, c, 2).wait_recv()
+
+                def units(r, _):
+                    some = rows_of(r)
+                    pre = mm(act[some], flat_fc[s]) + fcb[s]
+                    back = mm(gbuf[slot, part_of(r, QB)], flat_out[s])
+                    square = pre * pre
+                    tangent = jnp.tanh(pre * (GELU_C + (GELU_C * 0.044715) * square))
+                    half = 0.5 * pre
+                    fired[some] = (half + half * tangent).astype(bf16)
+                    slope = (0.5 + 0.5 * tangent) + half * (1.0 - tangent * tangent) * (
+                        GELU_C + (3.0 * GELU_C * 0.044715) * square
+                    )
+                    preg[some] = (back * slope).astype(bf16)
+                    return 0
+
+                lax.fori_loop(0, size // QB, units, 0)
+                oacc[all_rows] += mm(fired[all_rows], flat_out[s], NT)
+                gacc[all_rows] += mm(preg[all_rows], flat_fc[s], NT)
+
+                @pl.when(s == m)
+                def _():
+                    def outer(r, _):
+                        some = rows_of(r)
+                        dw[0, some] += mm(act[all_rows, some], preg[all_rows], TN)
+                        dw[1, some] += mm(gbuf[slot, g_rows, some], fired[all_rows], TN)
+                        return 0
+
+                    lax.fori_loop(0, 3, outer, 0)
+                    pgrad[6:7] += jnp.sum(preg[all_rows].astype(f32), axis=0, keepdims=True)
+
+                def at(when, do, *what):
+                    @pl.when(when)
+                    def _():
+                        for item in what:
+                            do(item)
+
+                if big:
+
+                    @pl.when((t == 0) & (s == 0))
+                    def _():
+                        advance(2, 2)
+
+                    @pl.when((t == 0) & (s == jnp.where(m == 3, 1, 2)))
+                    def _():
+                        advance(3, 2)
+
+                    @pl.when((t == 0) & (s == 2))
+                    def _():
+                        a_step(2, 1)
+                        a_step(1, 1)
+
+                    j = 4 * b + 4
+                    at((t >= 1) & (s == 0), stage_two, j + 3, j + 2)
+                    at((t >= 1) & (s == 2), stage_two, j + 1, j)
+                    at((t >= 1) & (s == 3), stage_three, j + 3, j + 2)
+                    at((t >= 2) & (s == 1), stage_four, j + 7, j + 6, j + 5, j + 4)
+                else:
+                    at((t == 0) & (s == 1), stage_two, 7, 6)
+                    at((t == 0) & (s == 3), stage_two, 5)
+                    at((t == 0) & (s == 2), stage_four, 11, 10, 9, 8)
+                    at((t == 1) & (s == 1), stage_three, 5)
+                    at((t == 1) & (s == 3), stage_three, 4)
+                return 0
+
+            lax.fori_loop(0, 4, slab, 0)
+            if big:
+
+                @pl.when(t == 0)
+                def _():
+                    a_step(2, 2)
+                    a_step(0, 1)
+
+            else:
+
+                @pl.when(t == 1)
+                def _():
+                    for c in range(3):
+                        for s in range(4):
+                            passed_on(*z_args(c, s))
+                            for stage in range(3):
+                                hop(s, c, stage).wait_send()
+                    for device in (x_dev, y_dev, diag, twin):
+                        pl.semaphore_signal(free, inc=1, device_id=device, device_id_type=MESH)
+                    give_twin(0)
+                    pl.semaphore_wait(free, 4)
+                    twin_sum(0).start()
+
+            def rejoin(r, _):
+                some = rows_of(r, RB)
+                there = pl.ds(pl.multiple_of(row + r * RB, RB), RB)
+                grad = gbuf[slot, part_of(r, RB)].astype(f32)
+                through, unit = gacc[some], normed[some]
+                pgrad[5:6] += jnp.sum(grad, axis=0, keepdims=True)
+                pgrad[2:3] += jnp.sum(through * unit, axis=0, keepdims=True)
+                pgrad[3:4] += jnp.sum(through, axis=0, keepdims=True)
+                branch = (grad + norm_back(through, par[2:3], unit, inv[some])).astype(bf16)
+                hid[there] = branch
+                pgrad[4:5] += jnp.sum(branch.astype(f32), axis=0, keepdims=True)
+                gbuf[slot, part_of(r, RB)] = oacc[some].astype(bf16)
+                return 0
+
+            lax.fori_loop(0, size // RB, rejoin, 0)
+            if big:
+                out_copy(b, slot).start()
+            else:
+                out_half(1 - t).start()
+            dwp[...] += mm(hid[rows], orow[rows], TN)
+            if not big:
+
+                @pl.when(t == 1)
+                def _():
+                    give_twin(2)
+                    twin_sum(2).start()
+                    give_owners(0)
+
+            rowg[all_rows] = mm(hid[rows], flat_pr[m]).astype(bf16)
+
+            for n in range(size // QB):
+                i = i_last - n
+                some = slice(size - QB * (n + 1), size - QB * n)
+                attend_block_back(
+                    i, rowg[some], qr, kr, vr, turned, orow, starts, lse, dk, dv, qs, gs, dqt
+                )
+                stacked[some, :WIDE] = (dqt[...].T * SCALE).astype(bf16)
+                stacked[some, WIDE : 2 * WIDE] = dk[rows_of(i)].astype(bf16)
+                stacked[some, 2 * WIDE :] = dv[rows_of(i)].astype(bf16)
+                whole = mm(stacked[some], flat_qkv[...], NT).astype(bf16)
+                part[2 * i] = whole[:RB]
+                part[2 * i + 1] = whole[RB:]
+
+                @pl.when(end)
+                def _():
+                    hop_a(2 * i + 1).start()
+                    hop_a(2 * i).start()
+
+                if big and n == 0:
+
+                    @pl.when(t >= 1)
+                    def _():
+                        stage_three(4 * b + 5)
+                        stage_three(4 * b + 4)
+
+                if not big:
+
+                    @pl.when(t == 0)
+                    def _():
+                        stage_two(4)
+                        stage_three(7)
+                        stage_three(6)
+
+                    @pl.when(t == 1)
+                    def _():
+                        stage_two(3)
+                        stage_two(2)
+
+            pgrad[7:8] += jnp.sum(stacked[all_rows].astype(f32), axis=0, keepdims=True)
+
+            def again(r, _):
+                unit, _ = norm(tokens[pl.ds(pl.multiple_of(row + r * RB, RB), RB)].astype(f32))
+                act[rows_of(r, RB)] = (unit * par[0:1] + par[1:2]).astype(bf16)
+                grad = part[row // RB + r].astype(f32)
+                pgrad[0:1] += jnp.sum(grad * unit, axis=0, keepdims=True)
+                pgrad[1:2] += jnp.sum(grad, axis=0, keepdims=True)
+                return 0
+
+            lax.fori_loop(0, size // RB, again, 0)
+
+            def outer(r, _):
+                some = rows_of(r)
+                dw[2, some] += mm(act[all_rows, some], stacked[all_rows], TN)
+                return 0
+
+            lax.fori_loop(0, 3, outer, 0)
+            if big:
+
+                @pl.when(t == 0)
+                def _():
+                    a_step(1, 2)
+
+                @pl.when(t == 1)
+                def _():
+                    a_step(0, 2)
+
             return 0
 
-        oacc[...] = tokens[rows].astype(f32) + par[4:5]
-        lax.fori_loop(0, 4, head, 0)
-
-        def second(r, _):
-            some = rows_of(r, RB)
-            hidden = oacc[some]
-            unit, inverse = norm(hidden)
-            normed[some] = unit
-            inv[some] = inverse
-            act[some] = (unit * par[2:3] + par[3:4]).astype(bf16)
-            oacc[some] = hidden + par[5:6]
-            gacc[some] = jnp.zeros_like(hidden)
-            return 0
-
-        lax.fori_loop(0, TB // RB, second, 0)
-
-        def slab(s, _):
-            def units(r, _):
-                some = rows_of(r)
-                pre = mm(act[some], flat_fc[s, :, 0:768]) + fcb[s]
-                back = mm(gbuf[slot, some], flat_out[s])
-                square = pre * pre
-                tangent = jnp.tanh(pre * (GELU_C + (GELU_C * 0.044715) * square))
-                half = 0.5 * pre
-                fired[some] = (half + half * tangent).astype(bf16)
-                slope = (0.5 + 0.5 * tangent) + half * (1.0 - tangent * tangent) * (
-                    GELU_C + (3.0 * GELU_C * 0.044715) * square
-                )
-                preg[some] = (back * slope).astype(bf16)
-                return 0
-
-            lax.fori_loop(0, TB // QB, units, 0)
-            oacc[...] += mm(fired[...], flat_out[s], NT)
-            gacc[...] += mm(preg[...], flat_fc[s, :, 0:768], NT)
-
-            @pl.when(s == m)
-            def _():
-                def outer(r, _):
-                    some = rows_of(r)
-                    dw[0, some] += mm(act[:, some], preg[...], TN)
-                    dw[1, some] += mm(gbuf[slot, :, some], fired[...], TN)
-                    return 0
-
-                lax.fori_loop(0, 3, outer, 0)
-                pgrad[6:7] += jnp.sum(preg[...].astype(f32), axis=0, keepdims=True)
-
-            @pl.when((s == 1) & (t >= 2))
-            def _():
-                stage_three(2 * b + 5)
-                stage_three(2 * b + 4)
-
-            return 0
-
-        lax.fori_loop(0, 4, slab, 0)
-
-        def rejoin(r, _):
-            some = rows_of(r, RB)
-            there = pl.ds(pl.multiple_of(b * TB + r * RB, RB), RB)
-            grad = gbuf[slot, some].astype(f32)
-            through, unit = gacc[some], normed[some]
-            pgrad[5:6] += jnp.sum(grad, axis=0, keepdims=True)
-            pgrad[2:3] += jnp.sum(through * unit, axis=0, keepdims=True)
-            pgrad[3:4] += jnp.sum(through, axis=0, keepdims=True)
-            branch = (grad + norm_back(through, par[2:3], unit, inv[some])).astype(bf16)
-            hid[there] = branch
-            pgrad[4:5] += jnp.sum(branch.astype(f32), axis=0, keepdims=True)
-            gbuf[slot, some] = oacc[some].astype(bf16)
-            return 0
-
-        lax.fori_loop(0, TB // RB, rejoin, 0)
-        out_copy(b, slot).start()
-        dwp[...] += mm(hid[rows], orow[rows], TN)
-        rowg[...] = mm(hid[rows], flat_fc[m, :, 768:1024]).astype(bf16)
-
-        @pl.when(t >= 1)
-        def _():
-            stage_two(2 * b + 3)
-            stage_two(2 * b + 2)
-
-        for half in (1, 0):
-            i = 2 * b + half
-            some = slice(half * QB, half * QB + QB)
-            attend_block_back(
-                i, rowg[some], qr, kr, vr, turned, orow, starts, lse, dk, dv, qs, gs, dqt
-            )
-            stacked[some, :WIDE] = (dqt[...].T * SCALE).astype(bf16)
-            stacked[some, WIDE : 2 * WIDE] = dk[rows_of(i)].astype(bf16)
-            stacked[some, 2 * WIDE :] = dv[rows_of(i)].astype(bf16)
-            part[i] = mm(stacked[some], flat_qkv[...], NT).astype(bf16)
-
-            @pl.when(end)
-            def _():
-                hop_a(i).start()
-
-        pgrad[7:8] += jnp.sum(stacked[...].astype(f32), axis=0, keepdims=True)
-        def again(r, _):
-            act[rows_of(r, RB)] = first_act(pl.ds(pl.multiple_of(b * TB + r * RB, RB), RB))
-            return 0
-
-        lax.fori_loop(0, TB // RB, again, 0)
-
-        def outer(r, _):
-            some = rows_of(r)
-            dw[2, some] += mm(act[:, some], stacked[...], TN)
-            return 0
-
-        lax.fori_loop(0, 3, outer, 0)
-
-        @pl.when(t >= 2)
-        def _():
-            stage_four(2 * b + 5)
-            stage_four(2 * b + 4)
-
-        return 0
-
-    lax.fori_loop(0, blocks, block, 0)
-
-    for c in range(2):
-        for o in range(3):
-            z_send[c][o].wait_send()
-        for o in range(4):
-            for stage in range(3):
-                hop(o, c, stage).wait_send()
-    for device in (x_dev, y_dev, diag, twin):
-        pl.semaphore_signal(free, inc=1, device_id=device, device_id_type=MESH)
-    sib = w_fc.at[:, :, :, 0, :, 0:768]
-
-    def rbuf(i):
-        return w_fc.at[:, i // 2, i % 2, 1, :, 0:768]
-
-    def pieces(yy, xx, kk):
-        return w_out.at[:, yy, xx, kk]
-
-    def take(c, dest):
-        if c < 3:
-            return dw[c, pl.ds(pl.multiple_of(dest * 96, 96), 96)]
-        return dwp[pl.ds(pl.multiple_of(dest * 96, 96), 96)]
-
-    spans = (768, 768, 768, 256)
-    for yy in range(2):
-        for xx in range(2):
-            for c in range(4):
-                w_out[c, yy, xx, 1 - k, :, : spans[c]] = take(c, yy * 4 + xx * 2 + 1 - k).astype(bf16)
-    twin_copy = remote(w_out.at[:, :, :, 1 - k], sib, d_s.at[0], d_r.at[0], twin)
-    pl.semaphore_wait(free, 4)
-    twin_copy.start()
-    stage_two(1)
+        return block
+
+    lax.fori_loop(0, blocks - 1, make_block(TB), 0)
+    lax.fori_loop(0, 2, make_block(QB), 0)
+
+    zg_send = [
+        remote(zgbuf.at[m], zgbuf.at[m], zg_s.at[o], zg_r.at[m], line[o]) for o in range(1, 4)
+    ]
+    zgbuf[m] = pgrad[...]
+    for copy in zg_send:
+        copy.start()
+    give_twin(1)
+    twin_sum(1).start()
     stage_three(3)
     stage_three(2)
-    twin_copy.wait_recv()
-    wants = [(y, 1 - x, x_dev), (1 - y, x, y_dev), (1 - y, 1 - x, diag)]
-    owner_copies = []
-    for i, (yy, xx, device) in enumerate(wants):
-        for c in range(4):
-            w_out[c, yy, xx, k, :, : spans[c]] = (
-                take(c, yy * 4 + xx * 2 + k) + w_fc[c, yy, xx, 0, :, : spans[c]].astype(f32)
-            ).astype(bf16)
-        copy = remote(pieces(yy, xx, k), rbuf(i), d_s.at[1 + i], d_r.at[1 + i], device)
-        copy.start()
-        owner_copies.append(copy)
-    stage_two(0)
-    stage_three(1)
-    stage_four(3)
-    stage_four(2)
-    stage_three(0)
-    for copy in owner_copies:
-        copy.wait_recv()
-    for c in range(4):
-        value = take(c, d) + w_fc[c, y, x, 0, :, : spans[c]].astype(f32)
-        for i in range(3):
-            value = value + w_fc[c, i // 2, i % 2, 1, :, : spans[c]].astype(f32)
-        if c < 3:
-            dw[c, pl.ds(pl.multiple_of(d * 96, 96), 96)] = value
-        else:
-            dwp[pl.ds(pl.multiple_of(d * 96, 96), 96)] = value
-    results = [
-        pltpu.make_async_copy(
-            dw.at[:, pl.ds(pl.multiple_of(d * 96, 96), 96)], dw_out, loc.at[3]
-        ),
-        pltpu.make_async_copy(dwp.at[pl.ds(pl.multiple_of(d * 96, 96), 96)], dwp_out, loc.at[4]),
-    ]
-    for copy in results:
-        copy.start()
-    stage_four(1)
-    stage_four(0)
-
+    for s in range(4):
+
+        @pl.when(m != s)
+        def _():
+            remote(zgbuf.at[s], zgbuf.at[s], zg_s.at[1], zg_r.at[s], line[1]).wait_recv()
+
+    pgrad[0:2] = zgbuf[0, 0:2] + zgbuf[1, 0:2] + zgbuf[2, 0:2] + zgbuf[3, 0:2]
     g_send = [
         remote(pgrad, pgbuf.at[o], g_s.at[o], g_r.at[o], plane[o]) for o in range(1, 8)
     ]
     for copy in g_send:
         copy.start()
+    give_owners(2)
+    give_owners(1)
+    for i in (7, 6, 5, 4):
+        stage_four(i)
+    stage_two(1)
+    stage_two(0)
     total = pgrad[...]
-    for o, copy in enumerate(g_send):
+    for copy in g_send:
         copy.wait_recv()
     for o in range(1, 8):
         total = total + pgbuf[o]
     pg_out[...] = total
-
-    for copy in results:
-        copy.wait()
-    for copy in g_send + q_send + q_pass + p_send + owner_copies + [twin_copy]:
+    stage_three(1)
+    stage_three(0)
+    stage_four(3)
+    stage_four(2)
+    own_sum(0)
+    own_sum(2)
+    own_sum(1)
+    stage_four(1)
+    stage_four(0)
+
+    for c in range(4):
+        result(c).wait()
+    for copy in g_send + zg_send + q_send + q_pass + p_send:
         copy.wait_send()
-    out_copy(0, (blocks - 1) % 2).wait()
+    for g in range(3):
+        twin_sum(g).wait_send()
+        for i in range(3):
+            to_owner(g, i).wait_send()
+    out_copy(1, (blocks - 2) % 2).wait()
+    out_half(1).wait()
+    out_half(0).wait()
 
     def leave(i, _):
         gt_out(i).wait()
@@ -966,13 +1188,15 @@
 
         return 0
 
-    lax.fori_loop(0, subs, leave, 0)
-    for b in range(blocks):
-        for o in range(1, 4):
-            a_send(b, o).wait_send()
-
-
-def whole_block(tokens, out_grad, starts, fc_own, out_own, qkv_own, par_own):
+    lax.fori_loop(0, count // RB, leave, 0)
+    for o in range(1, 4):
+        direct(blocks - 1, o).wait_send()
+    for b in range(blocks - 1):
+        for s in range(4):
+            passed_on(*a_args(b, s))
+
+
+def whole_block(tokens, out_grad, starts, fc_own, out_own, pr_own, qkv_own, par_own):
     count = tokens.shape[0]
     blocks, subs = count // TB, count // QB
     any_space = pl.BlockSpec(memory_space=pl.ANY)
@@ -986,11 +1210,12 @@
             jax.ShapeDtypeStruct((96, WIDE), f32),
             jax.ShapeDtypeStruct((8, 768), f32),
         ),
-        in_specs=[VMEM, any_space] + [VMEM] * 5,
+        in_specs=[VMEM, any_space] + [VMEM] * 6,
         out_specs=(any_space, any_space, any_space, any_space, VMEM),
         scratch_shapes=[
-            pltpu.VMEM((4, 2, 2, 2, 96, 1024), bf16),
             pltpu.VMEM((4, 2, 2, 2, 96, 768), bf16),
+            pltpu.VMEM((4, 2, 2, 2, 96, 768), bf16),
+            pltpu.VMEM((4, 2, 2, 2, 96, 256), bf16),
             pltpu.VMEM((2, 2, 2, 96, 768), bf16),
             pltpu.VMEM((8, 16, 768), bf16),
             pltpu.VMEM((16, 768), f32),
@@ -1023,32 +1248,36 @@
             pltpu.VMEM((768, 256), f32),
             pltpu.VMEM((8, 768), f32),
             pltpu.VMEM((8, 8, 768), f32),
-            pltpu.VMEM((subs, QB, 768), bf16),
-            pltpu.VMEM((subs, QB, 768), bf16),
-            pltpu.VMEM((subs, QB, 768), bf16),
+            pltpu.VMEM((4, 8, 768), f32),
+            pltpu.VMEM((count // RB, RB, 768), bf16),
+            pltpu.VMEM((count // RB, RB, 768), bf16),
+            pltpu.VMEM((count // RB, RB, 768), bf16),
             dma((7,)),
             dma((7,)),
             dma((8,)),
             dma((8,)),
-            dma((2, 4)),
-            dma((2, 4)),
-            dma((2, 3, 4)),
-            dma((2, 3, 4)),
+            dma((3, 4, 2)),
+            dma((3, 4)),
+            dma((3, 3, 4)),
+            dma((3, 3, 4)),
+            dma((4,)),
+            dma((blocks, 4, 2)),
             dma((blocks, 4)),
-            dma((blocks, 4)),
-            dma((3, subs)),
-            dma((3, subs)),
+            dma((3, count // RB)),
+            dma((3, count // RB)),
+            dma((12,)),
+            dma((12,)),
             dma((4,)),
             dma((4,)),
-            dma((8 + subs,)),
+            dma((8 + count // RB,)),
             dma((8,)),
-            dma((5,)),
+            dma((11,)),
             pltpu.SemaphoreType.REGULAR,
         ],
         compiler_params=pltpu.CompilerParams(
             collective_id=0, has_side_effects=True, vmem_limit_bytes=63 * 2**20
         ),
-    )(tokens, out_grad, starts, fc_own, out_own, qkv_own, par_own)
+    )(tokens, out_grad, starts, fc_own, out_own, pr_own, qkv_own, par_own)
 
 
 def per_device_whole(
@@ -1070,9 +1299,7 @@
 ):
     d = lax.axis_index("dp")
     starts = segment_starts(lengths[0], tokens.shape[0])
-    fc_own = jnp.concatenate(
-        [fc_weight, proj_weight.T, fc_bias.T, jnp.zeros((96, 63), bf16)], axis=1
-    )
+    pr_own = jnp.concatenate([proj_weight.T, fc_bias.T, jnp.zeros((96, 63), bf16)], axis=1)
     out_own = out_weight.T
     qkv_own = jnp.pad(qkv_weight, ((0, 0), (0, 0), (0, WIDE - 192)))
     qkv_own = jnp.moveaxis(qkv_own, 0, 1).reshape(96, 3 * WIDE)
@@ -1084,7 +1311,7 @@
     par_own = lax.dynamic_update_slice(par_own, qv_bias[0], (7, 24 * d))
     par_own = lax.dynamic_update_slice(par_own, qv_bias[1], (7, 2 * WIDE + 24 * d))
     output, grad_tokens, dw, dwp, pg = whole_block(
-        tokens, out_grad, starts, fc_own, out_own, qkv_own, par_own
+        tokens, out_grad, starts, fc_weight, out_own, pr_own, qkv_own, par_own
     )
     vec = lax.dynamic_slice(pg, (0, 96 * d), (7, 96))
     qv = jnp.concatenate(

time: 270 us -> 260 us (0.963)
  Pallas kernels: 247 us -> 238 us
    pallas_call x1, Pallas kernels: 247 us -> 238 us  [whole_block(): pl.pallas_call(whole_kernel, out_shape=(jax.ShapeDtypeStruct((count, 768)...]
where the time goes in v3:
time: 260 us; the launch traced here: 259 us
  Pallas kernels  238 us (92%)
  local copies, waits for them, and re-layouts  18.8 us (7%)
    pallas_call x1, Pallas kernels, whole_block(): pl.pallas_call(whole_kernel, out_shape=(jax.ShapeDtypeStruct((count, 768)...  238 us
    unnamed x12, local copies, waits for them, and re-layouts  8.03 us

profile of v3, /device:TPU:0, one launch (start us, length us, event | category | flops | bytes accessed | tf_op | source)
XLA Modules:
  0.0 259.4 jit_solution(15791943350625693110)
XLA Ops:
  0.7 0.8 stack.27
  1.4 0.3 dynamic_update_slice.9
  1.8 0.7 slice_bitcast_fusion.10
  2.6 0.2 dynamic_update_slice.11.par_own
  2.8 0.9 pad_bitcast_fusion
  3.7 0.7 copy.50
  4.4 0.9 copy.44
  5.3 0.8 copy.45
  6.2 0.7 maximum_maximum_fusion.pr_own
  6.9 0.7 copy.43
  7.8 0.7 select_reduce_fusion
  8.5 237.7 %shard_map.254 = (bf16[2048,768]{1,0:T(8,128)(2,1)}, bf16[2048,768]{1,0:T(8,128)(2,1)}, f32[3,96,768]{2,1,0:T(8,128)}, f32[96,256]{1,0:T(8,128)}, f32[8,768]{1,0:T(8,128)}) custom-call(bf16[2048,768]{1,0:T(8,128)(2,1)} %tokens.1, bf16[2048,768]{1,0:T(8,128)(2,1)} %grads.1, s32[1,2048]{1,0:T(1,128)} %bitcast.47, bf16[96,768]{1,0:T(8,128)(2,1)} %fc_own.1, ...), custom_call_target="tpu_custom_call" | custom-call | tf_op jit(solution)/shard_map/pallas_call | solution.py:1204
  246.2 0.9 constant_dynamic-slice_fusion.1
  247.1 0.6 pad_maximum_fusion
  247.7 0.8 constant_dynamic-slice_fusion.2
  248.5 0.5 slice_bitcast_fusion.4
  249.0 2.1 slice_bitcast_fusion.1
  251.1 1.1 reshape_squeeze.3
  252.3 0.8 copy.47
  253.0 0.9 slice_bitcast_fusion.3
  253.9 0.7 copy.49
  254.7 1.7 copy.56
  256.3 1.4 copy-done
  257.7 1.7 copy.57
  (12 shorter events, 0.4 us)
Async XLA Ops:
  2.8 5.7 %copy-start.2 = (bf16[16,768]{1,0:T(8,128)(2,1)}, bf16[16,768]{1,0:T(8,128)(2,1)S(1)}, u32[]{:S(2)}) copy-start(bf16[16,768]{1,0:T(8,128)(2,1)S(1)} %dynamic_update_slice.11.par_own) | copy-start | bytes 73732
  246.2 8.5 %copy-start.1 = (bf16[2048,768]{1,0:T(8,128)(2,1)S(1)}, bf16[2048,768]{1,0:T(8,128)(2,1)}, u32[]{:S(2)}) copy-start(bf16[2048,768]{1,0:T(8,128)(2,1)} %get-tuple-element.94) | copy-start | bytes 9437188
  254.7 3.0 %copy-start = (bf16[2048,768]{1,0:T(8,128)(2,1)S(1)}, bf16[2048,768]{1,0:T(8,128)(2,1)}, u32[]{:S(2)}) copy-start(bf16[2048,768]{1,0:T(8,128)(2,1)} %get-tuple-element.95) | copy-start | bytes 9437188

commit v4 on v3

--- a/solution.py
+++ b/solution.py
@@ -417,20 +417,31 @@
 def whole_kernel(
     tokens,
     grads,
-    starts,
+    lengths,
     fc_own,
     out_own,
     pr_own,
+    fb_own,
     qkv_own,
-    par_own,
+    gain_one,
+    shift_one,
+    gain_two,
+    shift_two,
+    proj_bias,
+    out_bias,
+    qv_own,
     output,
     grad_tokens,
-    dw_out,
-    dwp_out,
+    fc_grad,
+    out_grad,
+    qkv_grad,
+    pr_grad,
     pg_out,
     w_fc,
     w_out,
     w_pr,
+    starts,
+    par_own,
     w_qkv,
     pars,
     par,
@@ -515,13 +526,28 @@
     inner = jnp.logical_not(end)
     order = [m] + [jnp.where(m <= o - 1, o, o - 1) for o in range(1, 4)]
 
+    for c in range(3):
+        w_qkv[y, x, k, :, WIDE * c : WIDE * c + WIDE] = jnp.concatenate(
+            [qkv_own[c], jnp.zeros((96, WIDE - HPD * HD), bf16)], axis=1
+        )
+    par[...] = jnp.zeros_like(par)
+    vectors = (gain_one, shift_one, gain_two, shift_two, proj_bias, out_bias, fb_own)
+    for n, vector in enumerate(vectors):
+        par[n : n + 1, 0:96] = vector[...].astype(f32)
+    par[8:9, 0:24] = qv_own[0:1].astype(f32)
+    par[8:9, 2 * WIDE : 2 * WIDE + 24] = qv_own[1:2].astype(f32)
+    lined = pltpu.roll(par[0:8], 96 * d, 1)
+    heads = pltpu.roll(par[8:16], 24 * d, 1)
+    row = lax.broadcasted_iota(jnp.int32, (8, 768), 0)
+    lined = jnp.where(row == 7, jnp.broadcast_to(heads[0:1], (8, 768)), lined)
+    par_own[...] = jnp.concatenate([lined, jnp.zeros((8, 768), f32)], axis=0).astype(bf16)
     barrier = pltpu.get_barrier_semaphore()
     for device in plane[1:] + line[1:]:
         pl.semaphore_signal(barrier, inc=1, device_id=device, device_id_type=MESH)
     pl.semaphore_wait(barrier, 10)
 
     q_send = [
-        remote(qkv_own, w_qkv.at[y, x, k], q_s.at[i], q_r.at[i], device)
+        remote(w_qkv.at[y, x, k], w_qkv.at[y, x, k], q_s.at[i], q_r.at[i], device)
         for i, device in enumerate((x_dev, y_dev, diag, twin))
     ]
     q_from = [(y, 1 - x, k), (1 - y, x, k), (1 - y, 1 - x, k)]
@@ -536,8 +562,10 @@
         copy.start()
     w_fc[m, y, x, k] = fc_own[...]
     w_out[m, y, x, k] = out_own[...]
-    w_pr[m, y, x, k] = pr_own[...]
-    w_qkv[y, x, k] = qkv_own[...]
+    tall = jnp.concatenate(
+        [pr_own[...].astype(f32), fb_own[...].astype(f32), jnp.zeros((63, 96), f32)], axis=0
+    )
+    w_pr[m, y, x, k] = tall.T.astype(bf16)
     pars[0] = par_own[...]
     held = (w_fc, w_out, w_pr)
 
@@ -603,6 +631,14 @@
     for o in range(1, 8):
         total = total + pars[o].astype(f32)
     par[...] = total
+    spot = lax.broadcasted_iota(jnp.int32, (1, count), 1)
+    start = jnp.zeros((1, count), jnp.int32)
+    finish = lengths[0, 0]
+    for n in range(lengths.shape[1]):
+        start = jnp.where(spot >= finish, finish, start)
+        if n + 1 < lengths.shape[1]:
+            finish = finish + lengths[0, n + 1]
+    starts[...] = start
     dk[...] = jnp.zeros_like(dk)
     dv[...] = jnp.zeros_like(dv)
     dw[...] = jnp.zeros_like(dw)
@@ -832,27 +868,26 @@
                 ).astype(bf16)
             to_owner(g, i).start()
 
-    def result(c):
-        some = pl.ds(pl.multiple_of(d * 96, 96), 96)
-        return (
-            pltpu.make_async_copy(dw.at[c, some], dw_out.at[c], loc.at[7 + c])
-            if c < 3
-            else pltpu.make_async_copy(dwp.at[some], dwp_out, loc.at[10])
-        )
+    own_rows = pl.ds(pl.multiple_of(d * 96, 96), 96)
+    fc_result = pltpu.make_async_copy(dw.at[0, own_rows], fc_grad, loc.at[7])
 
     def own_sum(g):
         for i in range(3):
             to_owner(g, i).wait_recv()
-        some = pl.ds(pl.multiple_of(d * 96, 96), 96)
         for c in groups[g]:
             value = take(c, d) + w_fc[c, y, x, 0, :, : spans[c]].astype(f32)
             for i in range(3):
                 value = value + w_fc[c, i // 2, i % 2, 1, :, : spans[c]].astype(f32)
-            if c < 3:
-                dw[c, some] = value
+            if c == 0:
+                dw[0, own_rows] = value
+                fc_result.start()
+            elif c == 1:
+                out_grad[...] = value
+            elif c == 2:
+                for n in range(3):
+                    qkv_grad[n] = value[:, WIDE * n : WIDE * n + HPD * HD]
             else:
-                dwp[some] = value
-            result(c).start()
+                pr_grad[...] = value.T[: HPD * HD]
 
     def make_block(size):
         big = size == TB
@@ -1151,7 +1186,10 @@
         copy.wait_recv()
     for o in range(1, 8):
         total = total + pgbuf[o]
-    pg_out[...] = total
+    pg_out[0:8] = pltpu.roll(total, lax.rem(768 - 96 * d, 768), 1)[:, :128]
+    heads = pltpu.roll(total, lax.rem(768 - 24 * d, 768), 1)
+    pg_out[8:16] = heads[:, :128]
+    pg_out[16:24] = heads[:, 2 * WIDE : 2 * WIDE + 128]
     stage_three(1)
     stage_three(0)
     stage_four(3)
@@ -1162,8 +1200,7 @@
     stage_four(1)
     stage_four(0)
 
-    for c in range(4):
-        result(c).wait()
+    fc_result.wait()
     for copy in g_send + zg_send + q_send + q_pass + p_send:
         copy.wait_send()
     for g in range(3):
@@ -1196,7 +1233,7 @@
             passed_on(*a_args(b, s))
 
 
-def whole_block(tokens, out_grad, starts, fc_own, out_own, pr_own, qkv_own, par_own):
+def whole_block(tokens, out_grad, lengths, *shards):
     count = tokens.shape[0]
     blocks, subs = count // TB, count // QB
     any_space = pl.BlockSpec(memory_space=pl.ANY)
@@ -1206,16 +1243,20 @@
         out_shape=(
             jax.ShapeDtypeStruct((count, 768), bf16),
             jax.ShapeDtypeStruct((count, 768), bf16),
-            jax.ShapeDtypeStruct((3, 96, 768), f32),
-            jax.ShapeDtypeStruct((96, WIDE), f32),
-            jax.ShapeDtypeStruct((8, 768), f32),
+            jax.ShapeDtypeStruct((96, 768), f32),
+            jax.ShapeDtypeStruct((96, 768), f32),
+            jax.ShapeDtypeStruct((3, 96, HPD * HD), f32),
+            jax.ShapeDtypeStruct((HPD * HD, 96), f32),
+            jax.ShapeDtypeStruct((24, 128), f32),
         ),
-        in_specs=[VMEM, any_space] + [VMEM] * 6,
-        out_specs=(any_space, any_space, any_space, any_space, VMEM),
+        in_specs=[VMEM, any_space, pl.BlockSpec(memory_space=pltpu.SMEM)] + [VMEM] * len(shards),
+        out_specs=(any_space, any_space, any_space, VMEM, VMEM, VMEM, VMEM),
         scratch_shapes=[
             pltpu.VMEM((4, 2, 2, 2, 96, 768), bf16),
             pltpu.VMEM((4, 2, 2, 2, 96, 768), bf16),
             pltpu.VMEM((4, 2, 2, 2, 96, 256), bf16),
+            pltpu.VMEM((1, count), jnp.int32),
+            pltpu.VMEM((16, 768), bf16),
             pltpu.VMEM((2, 2, 2, 96, 768), bf16),
             pltpu.VMEM((8, 16, 768), bf16),
             pltpu.VMEM((16, 768), f32),
@@ -1277,7 +1318,7 @@
         compiler_params=pltpu.CompilerParams(
             collective_id=0, has_side_effects=True, vmem_limit_bytes=63 * 2**20
         ),
-    )(tokens, out_grad, starts, fc_own, out_own, pr_own, qkv_own, par_own)
+    )(tokens, out_grad, lengths, *shards)
 
 
 def per_device_whole(
@@ -1297,30 +1338,25 @@
     out_bias,
     out_grad,
 ):
-    d = lax.axis_index("dp")
-    starts = segment_starts(lengths[0], tokens.shape[0])
-    pr_own = jnp.concatenate([proj_weight.T, fc_bias.T, jnp.zeros((96, 63), bf16)], axis=1)
-    out_own = out_weight.T
-    qkv_own = jnp.pad(qkv_weight, ((0, 0), (0, 0), (0, WIDE - 192)))
-    qkv_own = jnp.moveaxis(qkv_own, 0, 1).reshape(96, 3 * WIDE)
-    vectors = jnp.stack(
-        [first_gain, first_shift, second_gain, second_shift, proj_bias, out_bias, fc_bias[0]]
-    )
-    par_own = jnp.zeros((16, 768), bf16)
-    par_own = lax.dynamic_update_slice(par_own, vectors, (0, 96 * d))
-    par_own = lax.dynamic_update_slice(par_own, qv_bias[0], (7, 24 * d))
-    par_own = lax.dynamic_update_slice(par_own, qv_bias[1], (7, 2 * WIDE + 24 * d))
-    output, grad_tokens, dw, dwp, pg = whole_block(
-        tokens, out_grad, starts, fc_weight, out_own, pr_own, qkv_own, par_own
-    )
-    vec = lax.dynamic_slice(pg, (0, 96 * d), (7, 96))
-    qv = jnp.concatenate(
-        [
-            lax.dynamic_slice(pg, (7, 24 * d), (1, 24)),
-            lax.dynamic_slice(pg, (7, 2 * WIDE + 24 * d), (1, 24)),
-        ]
-    )[:, None, :]
-    qkv_grad = jnp.moveaxis(dw[2].reshape(96, 3, WIDE)[:, :, :192], 1, 0)
+    output, grad_tokens, fc_grad, out_w_grad, qkv_grad, proj_grad, pg = whole_block(
+        tokens,
+        out_grad,
+        lengths,
+        fc_weight,
+        out_weight.T,
+        proj_weight,
+        fc_bias,
+        qkv_weight,
+        first_gain[None],
+        first_shift[None],
+        second_gain[None],
+        second_shift[None],
+        proj_bias[None],
+        out_bias[None],
+        qv_bias[:, 0],
+    )
+    vec = pg[:7, :96]
+    qv = jnp.concatenate([pg[15:16, :24], pg[23:24, :24]])[:, None, :]
     return (
         output,
         grad_tokens,
@@ -1328,13 +1364,13 @@
         vec[1],
         qkv_grad,
         qv,
-        dwp[:, :192].T,
+        proj_grad,
         vec[4],
         vec[2],
         vec[3],
-        dw[0],
+        fc_grad,
         vec[6][None],
-        dw[1].T,
+        out_w_grad.T,
         vec[5],
     )
 

time: 260 us -> 250 us (0.962)
  local copies, waits for them, and re-layouts: 18.8 us -> 10.5 us
    transpose x4 -> x0, local copies, waits for them, and re-layouts: 3.81 us -> none  [the longest x1 2.07 us: per_device_whole(): dw[1]]
    another operation x3 -> x0, local copies, waits for them, and re-layouts: 2.62 us -> none  [the longest x1 1.11 us: per_device_whole(): qkv_grad = jnp.moveaxis(dw[2].reshape(96, 3, WIDE)[:, :, :192], 1, 0)]
    unnamed x12 -> x16, local copies, waits for them, and re-layouts: 8.03 us -> 8.37 us
where the time goes in v4:
time: 250 us
  Pallas kernels  238 us (95%)
  local copies, waits for them, and re-layouts  10.5 us (4%)
    pallas_call x1, Pallas kernels, whole_block(): pl.pallas_call(whole_kernel, out_shape=(jax.ShapeDtypeStruct((count, 768)...  238 us
    unnamed x16, local copies, waits for them, and re-layouts  8.37 us

profile of v4, /device:TPU:0, one launch (start us, length us, event | category | flops | bytes accessed | tf_op | source)
XLA Modules:
  0.0 249.8 jit_solution(14654661967069820184)
XLA Ops:
  0.7 238.0 %shard_map.254 = (bf16[2048,768]{1,0:T(8,128)(2,1)}, bf16[2048,768]{1,0:T(8,128)(2,1)}, f32[96,768]{1,0:T(8,128)}, f32[96,768]{1,0:T(8,128)}, f32[3,96,192]{2,1,...) custom-call(bf16[2048,768]{1,0:T(8,128)(2,1)} %tokens.1, bf16[2048,768]{1,0:T(8,128)(2,1)} %grads.1, s32[1,16]{1,0:T(1,128)} %lengths.1, ...), custom_call_target="tpu_custom_call" | custom-call | tf_op jit(solution)/shard_map/pallas_call | solution.py:1241
  238.7 0.7 fusion
  239.4 0.6 pad_maximum_fusion
  239.9 1.5 slice_bitcast_fusion
  241.4 0.0 copy-start
  241.4 3.9 %copy.36 = bf16[2048,768]{1,0:T(8,128)(2,1)} copy(bf16[2048,768]{1,0:T(8,128)(2,1)} %get-tuple-element.65) | data formatting | bytes 6291456
  245.3 0.0 copy-done
  245.3 0.0 copy-start.3
  245.3 0.0 copy-start.4
  245.3 0.0 copy-start.2
  245.3 0.0 copy-start.1
  245.4 1.7 copy.37
  247.0 0.0 copy-done.3
  247.0 0.7 copy.38
  247.7 0.0 copy-done.4
  247.7 0.6 copy.39
  248.4 0.0 copy-done.2
  248.4 0.7 copy.40
  249.1 0.0 copy-done.1
  249.1 0.7 copy.41
Async XLA Ops:
  241.4 3.9 %copy-start = (bf16[2048,768]{1,0:T(8,128)(2,1)S(1)}, bf16[2048,768]{1,0:T(8,128)(2,1)}, u32[]{:S(2)}) copy-start(bf16[2048,768]{1,0:T(8,128)(2,1)} %get-tuple-element.66) | copy-start | bytes 9437188
  245.3 1.7 copy-start.3
  245.3 2.4 copy-start.4
  245.3 3.0 %copy-start.2 = (f32[96,768]{1,0:T(8,128)S(1)}, f32[96,768]{1,0:T(8,128)}, u32[]{:S(2)}) copy-start(f32[96,768]{1,0:T(8,128)} %get-tuple-element.75) | copy-start | bytes 884740
  245.3 3.8 %copy-start.1 = (f32[96,768]{1,0:T(8,128)S(1)}, f32[96,768]{1,0:T(8,128)}, u32[]{:S(2)}) copy-start(f32[96,768]{1,0:T(8,128)} %get-tuple-element.27) | copy-start | bytes 884740

commit v5 on v4

--- a/solution.py
+++ b/solution.py
@@ -927,7 +927,7 @@
                 def _():
                     a_wait(b, s)
 
-            def head(s, _):
+            def head(s):
                 third = rows_all[s, b, 2 * QB :].astype(f32)
                 turned_third = pltpu.roll(third, 64, 1)
                 if big:
@@ -937,11 +937,11 @@
                 lane = lax.broadcasted_iota(jnp.int32, third.shape, 1)
                 third = jnp.where(lane < 64, third, 0.0).astype(bf16)
                 left = jnp.concatenate([rows_all[s, b, g_rows], third], axis=1)
-                oacc[all_rows] += mm(left, flat_pr[s], NT)
-                return 0
-
-            oacc[all_rows] = tokens[rows].astype(f32) + par[4:5]
-            lax.fori_loop(0, 4, head, 0)
+                return mm(left, flat_pr[s], NT)
+
+            oacc[all_rows] = (
+                tokens[rows].astype(f32) + par[4:5] + (head(0) + head(1) + head(2) + head(3))
+            )
 
             def second(r, _):
                 some = rows_of(r, RB)

time: 250 us -> 247 us (0.988)
  Pallas kernels: 238 us -> 235 us
    pallas_call x1, Pallas kernels: 238 us -> 235 us  [whole_block(): pl.pallas_call(whole_kernel, out_shape=(jax.ShapeDtypeStruct((count, 768)...]
where the time goes in v5:
time: 247 us
  Pallas kernels  235 us (95%)
  local copies, waits for them, and re-layouts  10.5 us (4%)
    pallas_call x1, Pallas kernels, whole_block(): pl.pallas_call(whole_kernel, out_shape=(jax.ShapeDtypeStruct((count, 768)...  235 us
    unnamed x16, local copies, waits for them, and re-layouts  8.37 us

profile of v5, /device:TPU:0, one launch (start us, length us, event | category | flops | bytes accessed | tf_op | source)
XLA Modules:
  0.0 247.2 jit_solution(17288508662628264037)
XLA Ops:
  0.7 235.4 %shard_map.254 = (bf16[2048,768]{1,0:T(8,128)(2,1)}, bf16[2048,768]{1,0:T(8,128)(2,1)}, f32[96,768]{1,0:T(8,128)}, f32[96,768]{1,0:T(8,128)}, f32[3,96,192]{2,1,...) custom-call(bf16[2048,768]{1,0:T(8,128)(2,1)} %tokens.1, bf16[2048,768]{1,0:T(8,128)(2,1)} %grads.1, s32[1,16]{1,0:T(1,128)} %lengths.1, ...), custom_call_target="tpu_custom_call" | custom-call | tf_op jit(solution)/shard_map/pallas_call | solution.py:1241
  236.1 0.7 fusion
  236.8 0.6 pad_maximum_fusion
  237.4 1.5 slice_bitcast_fusion
  238.8 0.0 copy-start
  238.8 3.9 %copy.36 = bf16[2048,768]{1,0:T(8,128)(2,1)} copy(bf16[2048,768]{1,0:T(8,128)(2,1)} %get-tuple-element.65) | data formatting | bytes 6291456
  242.7 0.0 copy-done
  242.7 0.0 copy-start.3
  242.7 0.0 copy-start.4
  242.8 0.0 copy-start.2
  242.8 0.0 copy-start.1
  242.8 1.7 copy.37
  244.4 0.0 copy-done.3
  244.4 0.7 copy.38
  245.2 0.0 copy-done.4
  245.2 0.6 copy.39
  245.8 0.0 copy-done.2
  245.8 0.7 copy.40
  246.5 0.0 copy-done.1
  246.5 0.7 copy.41
Async XLA Ops:
  238.8 3.9 %copy-start = (bf16[2048,768]{1,0:T(8,128)(2,1)S(1)}, bf16[2048,768]{1,0:T(8,128)(2,1)}, u32[]{:S(2)}) copy-start(bf16[2048,768]{1,0:T(8,128)(2,1)} %get-tuple-element.66) | copy-start | bytes 9437188
  242.7 1.7 copy-start.3
  242.7 2.4 copy-start.4
  242.8 3.0 %copy-start.2 = (f32[96,768]{1,0:T(8,128)S(1)}, f32[96,768]{1,0:T(8,128)}, u32[]{:S(2)}) copy-start(f32[96,768]{1,0:T(8,128)} %get-tuple-element.75) | copy-start | bytes 884740
  242.8 3.8 %copy-start.1 = (f32[96,768]{1,0:T(8,128)S(1)}, f32[96,768]{1,0:T(8,128)}, u32[]{:S(2)}) copy-start(f32[96,768]{1,0:T(8,128)} %get-tuple-element.27) | copy-start | bytes 884740

commit v6 on v5

--- a/solution.py
+++ b/solution.py
@@ -467,7 +467,6 @@
     gacc,
     fired,
     preg,
-    rowg,
     stacked,
     hid,
     dw,
@@ -978,7 +977,7 @@
                     preg[some] = (back * slope).astype(bf16)
                     return 0
 
-                lax.fori_loop(0, size // QB, units, 0)
+                lax.fori_loop(0, size // QB, units, 0, unroll=True)
                 oacc[all_rows] += mm(fired[all_rows], flat_out[s], NT)
                 gacc[all_rows] += mm(preg[all_rows], flat_fc[s], NT)
 
@@ -1078,13 +1077,13 @@
                     twin_sum(2).start()
                     give_owners(0)
 
-            rowg[all_rows] = mm(hid[rows], flat_pr[m]).astype(bf16)
+            stacked[all_rows, :WIDE] = mm(hid[rows], flat_pr[m]).astype(bf16)
 
             for n in range(size // QB):
                 i = i_last - n
                 some = slice(size - QB * (n + 1), size - QB * n)
                 attend_block_back(
-                    i, rowg[some], qr, kr, vr, turned, orow, starts, lse, dk, dv, qs, gs, dqt
+                    i, stacked[some, :WIDE], qr, kr, vr, turned, orow, starts, lse, dk, dv, qs, gs, dqt
                 )
                 stacked[some, :WIDE] = (dqt[...].T * SCALE).astype(bf16)
                 stacked[some, WIDE : 2 * WIDE] = dk[rows_of(i)].astype(bf16)
@@ -1282,7 +1281,6 @@
             pltpu.VMEM((TB, 768), f32),
             pltpu.VMEM((TB, 768), bf16),
             pltpu.VMEM((TB, 768), bf16),
-            pltpu.VMEM((TB, WIDE), bf16),
             pltpu.VMEM((TB, 768), bf16),
             pltpu.VMEM((count, 768), bf16),
             pltpu.VMEM((3, 768, 768), f32),
@@ -1316,7 +1314,7 @@
             pltpu.SemaphoreType.REGULAR,
         ],
         compiler_params=pltpu.CompilerParams(
-            collective_id=0, has_side_effects=True, vmem_limit_bytes=63 * 2**20
+            collective_id=0, has_side_effects=True, vmem_limit_bytes=63 * 2**20 + 2**18
         ),
     )(tokens, out_grad, lengths, *shards)
 

time: 247 us -> 244 us (0.988)
  Pallas kernels: 235 us -> 232 us
    pallas_call x1, Pallas kernels: 235 us -> 232 us  [whole_block(): pl.pallas_call(whole_kernel, out_shape=(jax.ShapeDtypeStruct((count, 768)...]
where the time goes in v6:
time: 244 us
  Pallas kernels  232 us (95%)
  local copies, waits for them, and re-layouts  10.5 us (4%)
    pallas_call x1, Pallas kernels, whole_block(): pl.pallas_call(whole_kernel, out_shape=(jax.ShapeDtypeStruct((count, 768)...  232 us
    unnamed x16, local copies, waits for them, and re-layouts  8.37 us

profile of v6, /device:TPU:0, one launch (start us, length us, event | category | flops | bytes accessed | tf_op | source)
XLA Modules:
  0.0 244.1 jit_solution(8655405916876847479)
XLA Ops:
  0.7 232.3 %shard_map.254 = (bf16[2048,768]{1,0:T(8,128)(2,1)}, bf16[2048,768]{1,0:T(8,128)(2,1)}, f32[96,768]{1,0:T(8,128)}, f32[96,768]{1,0:T(8,128)}, f32[3,96,192]{2,1,...) custom-call(bf16[2048,768]{1,0:T(8,128)(2,1)} %tokens.1, bf16[2048,768]{1,0:T(8,128)(2,1)} %grads.1, s32[1,16]{1,0:T(1,128)} %lengths.1, ...), custom_call_target="tpu_custom_call" | custom-call | tf_op jit(solution)/shard_map/pallas_call | solution.py:1240
  233.0 0.7 fusion
  233.6 0.6 pad_maximum_fusion
  234.2 1.5 slice_bitcast_fusion
  235.7 0.0 copy-start
  235.7 3.9 %copy.36 = bf16[2048,768]{1,0:T(8,128)(2,1)} copy(bf16[2048,768]{1,0:T(8,128)(2,1)} %get-tuple-element.65) | data formatting | bytes 6291456
  239.6 0.0 copy-done
  239.6 0.0 copy-start.3
  239.6 0.0 copy-start.4
  239.6 0.0 copy-start.2
  239.6 0.0 copy-start.1
  239.6 1.7 copy.37
  241.3 0.0 copy-done.3
  241.3 0.7 copy.38
  242.0 0.0 copy-done.4
  242.0 0.6 copy.39
  242.7 0.0 copy-done.2
  242.7 0.7 copy.40
  243.4 0.0 copy-done.1
  243.4 0.7 copy.41
Async XLA Ops:
  235.7 3.9 %copy-start = (bf16[2048,768]{1,0:T(8,128)(2,1)S(1)}, bf16[2048,768]{1,0:T(8,128)(2,1)}, u32[]{:S(2)}) copy-start(bf16[2048,768]{1,0:T(8,128)(2,1)} %get-tuple-element.66) | copy-start | bytes 9437188
  239.6 1.7 copy-start.3
  239.6 2.4 copy-start.4
  239.6 3.0 %copy-start.2 = (f32[96,768]{1,0:T(8,128)S(1)}, f32[96,768]{1,0:T(8,128)}, u32[]{:S(2)}) copy-start(f32[96,768]{1,0:T(8,128)} %get-tuple-element.75) | copy-start | bytes 884740
  239.6 3.8 %copy-start.1 = (f32[96,768]{1,0:T(8,128)S(1)}, f32[96,768]{1,0:T(8,128)}, u32[]{:S(2)}) copy-start(f32[96,768]{1,0:T(8,128)} %get-tuple-element.27) | copy-start | bytes 884740
